TPU v7x, 128 devices: a whole 4x4x4 slice. The times are simulated.
128 devices in a mesh: dp: 32 (over y, x_hi, z), tensor: 4 (over x_lo, core).
Axes of the slice: x: 4 (x_hi: 2, x_lo: 2; x = x_hi * 2 + x_lo), y: 4, z: 4, core: 2. Of those that a mesh axis runs over, the one named last changes fastest.
Arguments:
- tokens: bfloat16 [12288, 2048], P('dp'), may hold values from -6 to 6
- seq_lengths: int32 [128], P('dp'), may hold values from 0 to 384, as said below
- attention_gain: float32 [2048], replicated, may hold values from 0.1 to 1.9
- feedforward_gain: float32 [2048], replicated, may hold values from 0.1 to 1.9
- query_weight: bfloat16 [2048, 2048], P('dp', 'tensor'), may hold values from -0.125 to 0.125
- key_weight: bfloat16 [2048, 2048], P('dp', 'tensor'), may hold values from -0.125 to 0.125
- value_weight: bfloat16 [2048, 2048], P('dp', 'tensor'), may hold values from -0.125 to 0.125
- output_weight: bfloat16 [2048, 2048], P('tensor', 'dp'), may hold values from -0.75 to 0.75
- gate_weight: bfloat16 [2048, 8192], P('dp', 'tensor'), may hold values from -0.125 to 0.125
- up_weight: bfloat16 [2048, 8192], P('dp', 'tensor'), may hold values from -0.125 to 0.125
- down_weight: bfloat16 [8192, 2048], P('tensor', 'dp'), may hold values from -0.0625 to 0.0625
- cotangent: bfloat16 [12288, 2048], P('dp'), may hold values from -6 to 6
Outputs:
- layer_out: bfloat16 [12288, 2048], P('dp')
- tokens_grad: float32 [12288, 2048], P('dp')
- attention_gain_grad: float32 [2048], replicated
- feedforward_gain_grad: float32 [2048], replicated
- query_grad: float32 [2048, 2048], P('dp', 'tensor')
- key_grad: float32 [2048, 2048], P('dp', 'tensor')
- value_grad: float32 [2048, 2048], P('dp', 'tensor')
- output_grad: float32 [2048, 2048], P('tensor', 'dp')
- gate_grad: float32 [2048, 8192], P('dp', 'tensor')
- up_grad: float32 [2048, 8192], P('dp', 'tensor')
- down_grad: float32 [8192, 2048], P('tensor', 'dp')
Inputs may be any that keep to these rules, and one draw needn't show every extreme that they name: `seq_lengths`: each device's 4 lengths sum to between 192 and 384; lengths may be 0; in every draw some device holds a single sequence of 384 rows.
All inputs are finite; a program needn't handle non-finite values.
Results may differ from a plain program's by a relative error of at most 0.025.
Values may be sent and summed in bfloat16 or wider, within the bound.
No kernel may reach another device: no remote copies, remote signals or barrier semaphores. Data moves between devices by JAX's collectives and lax.ppermute only.
A program may use at most 192 MiB of HBM per device.

v0:
```python
import jax
import jax.numpy as jnp
from jax import lax
from jax.sharding import PartitionSpec as P

HEAD = 64


norm_epsilon = 1e-05
rope_base = 130000.0
masked_score = -1000000000.0


def turned_gather(arrays, axis, dims):
    turned = [jnp.moveaxis(a, dim, 0) for a, dim in zip(arrays, dims)]
    widths = [t[0].size for t in turned]
    both = jnp.concatenate([t.reshape(-1, w) for t, w in zip(turned, widths)], axis=1)
    result = lax.all_gather(both, axis, axis=0, tiled=True)
    blocks = jnp.split(result, [sum(widths[:k]) for k in range(1, len(widths))], axis=1)
    return tuple(
        (
            jnp.moveaxis(b.reshape(-1, *t.shape[1:]), 0, dim)
            for b, t, dim in zip(blocks, turned, dims)
        )
    )


def side_by_side(arrays, axis, dim, along):
    widths = [a.shape[along] for a in arrays]
    both = jnp.concatenate(arrays, axis=along)
    result = lax.psum_scatter(both, axis, scatter_dimension=dim, tiled=True)
    return tuple(jnp.split(result, [sum(widths[:k]) for k in range(1, len(widths))], axis=along))


def copy_for_each(value, axis):
    size = lax.axis_size(axis)
    return lax.all_to_all(
        jnp.broadcast_to(value[None], (size, *value.shape)), axis, 0, 0, tiled=True
    )


def of_everyone(value, axis):
    return copy_for_each(value, axis).sum(axis=0)


def in_one(arrays, axis):
    ends = [0]
    for a in arrays:
        ends.append(ends[-1] + a.size)
    subtotal = of_everyone(jnp.concatenate([a.ravel() for a in arrays]), axis)
    return tuple((subtotal[b:e].reshape(a.shape) for a, b, e in zip(arrays, ends, ends[1:])))


def layout(lengths, rows):
    ends = jnp.cumsum(lengths)
    places = jnp.arange(rows, dtype=jnp.int32)
    passed = places[:, None] >= ends[None, :]
    segment = jnp.sum(passed.astype(jnp.int32), axis=1)
    begins = jnp.max(jnp.where(passed, ends[None, :], jnp.zeros_like(ends)[None, :]), axis=1)
    return (segment, places - begins)


def rotary(position):
    index = jnp.arange(HEAD // 2, dtype=jnp.float32)
    frequency = rope_base ** (-2.0 * index / HEAD)
    angle = position.astype(jnp.float32)[:, None] * frequency[None, :]
    return (jnp.cos(angle)[:, None, :], jnp.sin(angle)[:, None, :])


def rotate(values, cosine, sine):
    half = values.shape[-1] // 2
    first, second = (values[..., :half], values[..., half:])
    return jnp.concatenate(
        [first * cosine - second * sine, second * cosine + first * sine], axis=-1
    )


def rotate_back(grads, cosine, sine):
    half = grads.shape[-1] // 2
    first, second = (grads[..., :half], grads[..., half:])
    return jnp.concatenate(
        [first * cosine + second * sine, second * cosine - first * sine], axis=-1
    )


def local_dot(left, right):
    return jnp.dot(left, right, preferred_element_type=jnp.float32)


def dot_right_t(left, right):
    return lax.dot_general(
        left, right, (((1,), (1,)), ((), ())), preferred_element_type=jnp.float32
    )


def dot_left_t(left, right):
    return lax.dot_general(
        left, right, (((0,), (0,)), ((), ())), preferred_element_type=jnp.float32
    )


def masked_scores(query_rot, key_rot, allowed):
    scores = jnp.einsum("qhd,khd->hqk", query_rot, key_rot, preferred_element_type=jnp.float32)
    return jnp.where(allowed[None], scores, masked_score)


def per_device(
    tokens,
    seq_lengths,
    attention_gain,
    feedforward_gain,
    query_weight,
    key_weight,
    value_weight,
    output_weight,
    gate_weight,
    up_weight,
    down_weight,
    cotangent,
):
    rows = tokens.shape[0]
    hidden = tokens.astype(jnp.float32)
    segment, position = layout(seq_lengths, rows)
    places = jnp.arange(rows, dtype=jnp.int32)
    allowed = (segment[:, None] == segment[None, :]) & (places[:, None] >= places[None, :])
    cosine, sine = rotary(position)
    head_scale = HEAD ** (-0.5)
    attention_full = turned_gather(
        (query_weight, key_weight, value_weight, output_weight), "dp", (0, 0, 0, 1)
    )
    query_full, key_full, value_full, output_full = attention_full
    heads_local = query_full.shape[1] // HEAD
    scale_one = lax.rsqrt(jnp.mean(hidden * hidden, axis=-1, keepdims=True) + norm_epsilon)
    hidden_unit = hidden * scale_one
    normed_one = (hidden_unit * attention_gain).astype(jnp.bfloat16)
    query_pre = local_dot(normed_one, query_full).reshape(rows, heads_local, HEAD)
    query_rot = (rotate(query_pre, cosine, sine) * head_scale).astype(jnp.bfloat16)
    key_pre = local_dot(normed_one, key_full).reshape(rows, heads_local, HEAD)
    key_rot = rotate(key_pre, cosine, sine).astype(jnp.bfloat16)
    value_low = (
        local_dot(normed_one, value_full).astype(jnp.bfloat16).reshape(rows, heads_local, HEAD)
    )
    scores = masked_scores(query_rot, key_rot, allowed)
    top_score = jnp.max(scores, axis=-1, keepdims=True)
    log_total = top_score + jnp.log(jnp.sum(jnp.exp(scores - top_score), axis=-1, keepdims=True))
    weights_low = jnp.exp(scores - log_total).astype(jnp.bfloat16)
    attended = jnp.einsum(
        "hqk,khd->qhd", weights_low, value_low, preferred_element_type=jnp.float32
    )
    attended = attended.reshape(rows, -1).astype(jnp.bfloat16)
    branch = lax.psum(local_dot(attended, output_full), "tensor")
    middle = hidden + branch
    scale_two = lax.rsqrt(jnp.mean(middle * middle, axis=-1, keepdims=True) + norm_epsilon)
    middle_unit = middle * scale_two
    normed_two = (middle_unit * feedforward_gain).astype(jnp.bfloat16)
    feed_full = turned_gather((gate_weight, up_weight, down_weight), "dp", (0, 0, 1))
    gate_full, up_full, down_full = feed_full
    gate_value = local_dot(normed_two, gate_full)
    up_value = local_dot(normed_two, up_full)
    sigmoid_gate = jax.nn.sigmoid(gate_value)
    silu_gate = gate_value * sigmoid_gate
    mixed_low = (silu_gate * up_value).astype(jnp.bfloat16)
    feed_branch = lax.psum(local_dot(mixed_low, down_full).astype(jnp.bfloat16), "tensor").astype(
        jnp.float32
    )
    layer_out = (middle + feed_branch).astype(jnp.bfloat16)
    out_grad = cotangent.astype(jnp.float32)
    feed_back = turned_gather((gate_weight, up_weight, down_weight), "dp", (0, 0, 1))
    gate_back, up_back, down_back = feed_back
    mixed_grad = dot_right_t(cotangent, down_back)
    gate_grad_low = (
        mixed_grad * up_value * sigmoid_gate * (1.0 + gate_value * (1.0 - sigmoid_gate))
    ).astype(jnp.bfloat16)
    up_grad_low = (mixed_grad * silu_gate).astype(jnp.bfloat16)
    feed_input = dot_right_t(gate_grad_low, gate_back) + dot_right_t(up_grad_low, up_back)
    down_term = dot_left_t(mixed_low, cotangent)
    gate_term = dot_left_t(normed_two, gate_grad_low)
    up_term = dot_left_t(normed_two, up_grad_low)
    gate_grad, up_grad, down_grad = (
        *tuple(
            (
                part.astype(jnp.float32)
                for part in side_by_side(
                    (gate_term.astype(jnp.bfloat16), up_term.astype(jnp.bfloat16)), "dp", 0, 1
                )
            )
        ),
        lax.psum_scatter(
            down_term.astype(jnp.bfloat16), "dp", scatter_dimension=1, tiled=True
        ).astype(jnp.float32),
    )
    normed_two_grad = lax.psum(feed_input, "tensor")
    weighted_two = normed_two_grad * feedforward_gain
    middle_grad = out_grad + scale_two * (
        weighted_two - middle_unit * jnp.mean(weighted_two * middle_unit, axis=-1, keepdims=True)
    )
    gain_two_part = jnp.sum(normed_two_grad * middle_unit, axis=0)
    middle_grad_low = middle_grad.astype(jnp.bfloat16)
    attention_back = turned_gather(
        (query_weight, key_weight, value_weight, output_weight), "dp", (0, 0, 0, 1)
    )
    query_back, key_back, value_back, output_back = attention_back
    output_term = dot_left_t(attended, middle_grad_low)
    attended_grad = (
        dot_right_t(middle_grad_low, output_back)
        .astype(jnp.bfloat16)
        .reshape(rows, heads_local, HEAD)
    )
    scores_again = masked_scores(query_rot, key_rot, allowed)
    probs = jnp.exp(scores_again - log_total)
    probs_low = probs.astype(jnp.bfloat16)
    prob_grad = jnp.einsum(
        "qhd,khd->hqk", attended_grad, value_low, preferred_element_type=jnp.float32
    )
    score_grad = (probs * (prob_grad - jnp.sum(probs * prob_grad, axis=-1, keepdims=True))).astype(
        jnp.bfloat16
    )
    value_grad_low = jnp.einsum(
        "hqk,qhd->khd", probs_low, attended_grad, preferred_element_type=jnp.float32
    )
    value_grad_low = value_grad_low.astype(jnp.bfloat16).reshape(rows, -1)
    query_grad_rot = jnp.einsum(
        "hqk,khd->qhd", score_grad, key_rot, preferred_element_type=jnp.float32
    )
    key_grad_rot = jnp.einsum(
        "hqk,qhd->khd", score_grad, query_rot, preferred_element_type=jnp.float32
    )
    query_pre_grad = (
        rotate_back(query_grad_rot * head_scale, cosine, sine)
        .astype(jnp.bfloat16)
        .reshape(rows, -1)
    )
    key_pre_grad = rotate_back(key_grad_rot, cosine, sine).astype(jnp.bfloat16).reshape(rows, -1)
    query_term = dot_left_t(normed_one, query_pre_grad)
    key_term = dot_left_t(normed_one, key_pre_grad)
    value_term = dot_left_t(normed_one, value_grad_low)
    attention_input = (
        dot_right_t(query_pre_grad, query_back)
        + dot_right_t(key_pre_grad, key_back)
        + dot_right_t(value_grad_low, value_back)
    )
    query_grad, key_grad, value_grad, output_grad = (
        *tuple(
            (
                part.astype(jnp.float32)
                for part in side_by_side(
                    (
                        query_term.astype(jnp.bfloat16),
                        key_term.astype(jnp.bfloat16),
                        value_term.astype(jnp.bfloat16),
                    ),
                    "dp",
                    0,
                    1,
                )
            )
        ),
        lax.psum_scatter(
            output_term.astype(jnp.bfloat16), "dp", scatter_dimension=1, tiled=True
        ).astype(jnp.float32),
    )
    normed_one_grad = lax.psum(attention_input.astype(jnp.bfloat16), "tensor").astype(jnp.float32)
    weighted_one = normed_one_grad * attention_gain
    tokens_grad = middle_grad + scale_one * (
        weighted_one - hidden_unit * jnp.mean(weighted_one * hidden_unit, axis=-1, keepdims=True)
    )
    gain_one_part = jnp.sum(normed_one_grad * hidden_unit, axis=0)
    gain_one_grad, gain_two_grad = in_one((gain_one_part, gain_two_part), "dp")
    return (
        layer_out,
        tokens_grad,
        gain_one_grad,
        gain_two_grad,
        query_grad,
        key_grad,
        value_grad,
        output_grad,
        gate_grad,
        up_grad,
        down_grad,
    )


def solution(mesh):
    return jax.shard_map(
        per_device,
        mesh=mesh,
        in_specs=(
            P("dp", None),
            P("dp"),
            P(),
            P(),
            P("dp", "tensor"),
            P("dp", "tensor"),
            P("dp", "tensor"),
            P("tensor", "dp"),
            P("dp", "tensor"),
            P("dp", "tensor"),
            P("tensor", "dp"),
            P("dp", None),
        ),
        out_specs=(
            P("dp", None),
            P("dp", None),
            P(),
            P(),
            P("dp", "tensor"),
            P("dp", "tensor"),
            P("dp", "tensor"),
            P("tensor", "dp"),
            P("dp", "tensor"),
            P("dp", "tensor"),
            P("tensor", "dp"),
        ),
        check_vma=False,
    )
```

profile of v0, /device:TPU:0, one launch (start us, length us, event | category | flops | bytes accessed | tf_op | source)
XLA Modules:
  0.0 1492.3 jit_solution(4885264739749941355)
XLA Ops:
  7.2 1.7 pad_maximum_fusion.6
  9.9 1.8 fusion.22
  12.1 105.9 %all-gather.3.cloned.1.call-done = bf16[2048,2048]{1,0:T(8,128)(2,1)} async-done(((bf16[64,2048]{1,0:T(8,128)(2,1)}), bf16[2048,2048]{1,0:T(8,128)(2,1)}) %all-gather.3.cloned.1.call-update) | async-done | bytes 8388624 | tf_op jit(solution)/shard_map/all_gather | solution.py:18
  118.0 3.1 fusion.51
  121.3 3.1 fusion.41
  124.5 3.0 fusion.45
  127.7 0.9 select_reduce_fusion
  128.6 0.8 exponential_reduce_fusion
  129.5 1.2 convolution_convert_fusion.8
  130.8 4.4 fusion.37
  135.3 0.9 copy-done.27
  136.3 1.0 pad_maximum_fusion.2
  137.5 70.2 %all-reduce.5.cloned.1.call-done = f32[384,2048]{1,0:T(8,128)} async-done(((f32[384,2048]{1,0:T(8,128)}), f32[384,2048]{1,0:T(8,128)}) %all-reduce.5.cloned.1.call-update) | async-done | bytes 3145744 | tf_op jit(solution)/shard_map/psum | solution.py:151
  207.7 2.8 multiply_reduce_fusion.3
  210.6 2.2 multiply_convert_fusion.2
  212.8 208.7 %all-gather.5.cloned.1.call-done = bf16[2048,6144]{1,0:T(8,128)(2,1)} async-done(((bf16[64,6144]{1,0:T(8,128)(2,1)}), bf16[2048,6144]{1,0:T(8,128)(2,1)}) %all-gather.5.cloned.1.call-update) | async-done | bytes 25165840 | tf_op jit(solution)/shard_map/all_gather | solution.py:18
  421.5 6.4 fusion
  427.9 5.9 fusion.10
  433.8 9.1 fusion.25
  442.9 7.0 fusion.4
  449.9 8.5 fusion.29
  458.7 8.6 fusion.32
  467.3 63.6 %all-reduce.7.cloned.1.call-done = f32[384,2048]{1,0:T(8,128)} async-done(((f32[384,2048]{1,0:T(8,128)}), f32[384,2048]{1,0:T(8,128)}) %all-reduce.7.cloned.1.call-update) | async-done | bytes 3145744 | tf_op jit(solution)/shard_map/psum | solution.py:192
  530.9 3.4 multiply_reduce_fusion.1
  534.4 0.9 multiply_add_fusion
  535.3 1.7 copy-done.1
  536.9 3.3 fusion.54
  540.3 1.9 copy.88
  542.2 3.8 convolution_convert_fusion.7
  546.0 3.9 multiply_reduce_fusion
  549.9 1.1 multiply_convert_fusion
  551.1 0.9 convolution_bitcast_fusion
  553.2 1.0 fusion.43
  554.3 1.5 fusion.39
  555.8 2.2 add_convert_fusion
  558.1 0.9 copy-done.6
  559.0 4.5 convolution_convert_fusion.6
  563.6 3.0 convolution_convert_fusion.3
  566.7 1.4 convolution_convert_fusion.4
  568.1 1.4 convolution_convert_fusion.5
  569.5 11.4 pad_maximum_fusion.1
  580.9 8.7 copy.105
  589.8 9.7 convolution_convert_fusion
  599.6 6.6 convolution_convert_fusion.2
  606.2 4.9 convolution_convert_fusion.1
  611.0 7.6 pad_maximum_fusion
  618.7 20.8 %copy.107 = bf16[2048,4096]{1,0:T(8,128)(2,1)} copy(bf16[2048,4096]{0,1:T(8,128)(2,1)} %pad_maximum_fusion) | data formatting | bytes 33554432
  639.6 3.0 fusion.21
  642.5 1.3 broadcast_in_dim.35
  643.8 9.7 all-to-all-start
  653.6 5.6 fusion.18
  659.1 1.7 add_convert_fusion.1
  660.8 6.2 all-to-all-done
  667.0 1.4 reduce_sum.99
  669.0 155.7 %reduce-scatter.9.cloned.1.call-done = bf16[512,64]{0,1:T(8,128)(2,1)} async-done(((bf16[512,2048]{0,1:T(8,128)(2,1)}), bf16[512,64]{0,1:T(8,128)(2,1)}) %reduce-scatter.9.cloned.1.call-update) | async-done | bytes 65552 | tf_op jit(solution)/shard_map/reduce_scatter | solution.py:258
  824.7 1.5 convert_element_type.167
  826.3 230.5 %reduce-scatter.13.cloned.1.call-done = bf16[64,1536]{1,0:T(8,128)(2,1)} async-done(((bf16[2048,1536]{1,0:T(8,128)(2,1)}), bf16[64,1536]{1,0:T(8,128)(2,1)}) %reduce-scatter.13.cloned.1.call-update) | async-done | bytes 196624
  1056.8 0.9 fusion.81
  1060.3 199.5 %reduce-scatter.11.cloned.1.call-done = bf16[2048,64]{0,1:T(8,128)(2,1)} async-done(((bf16[2048,2048]{0,1:T(8,128)(2,1)}), bf16[2048,64]{0,1:T(8,128)(2,1)}) %reduce-scatter.11.cloned.1.call-update) | async-done | bytes 262160 | tf_op jit(solution)/shard_map/reduce_scatter | solution.py:188
  1259.9 1.8 convert_element_type.173
  1261.7 220.2 %reduce-scatter.15.cloned.1.call-done = bf16[64,4096]{1,0:T(8,128)(2,1)} async-done(((bf16[2048,4096]{1,0:T(8,128)(2,1)}), bf16[64,4096]{1,0:T(8,128)(2,1)}) %reduce-scatter.15.cloned.1.call-update) | async-done | bytes 524304
  1481.9 1.1 fusion.80
  1483.2 1.0 copy.97
  1484.5 1.0 copy.96
  (130 shorter events, 8.2 us)
Async XLA Ops:
  7.2 110.8 %all-gather.3.cloned.1.call-start = ((), (), s32[]{:S(2)}) async-start(), calls=%async_computation.5 | async-start | bytes 8650752 | tf_op jit(solution)/shard_map/all_gather | solution.py:18
  8.9 198.8 %all-reduce.5.cloned.1.call-start = ((), (), s32[]{:S(2)}) async-start(), calls=%async_computation.6 | async-start | bytes 6291456 | tf_op jit(solution)/shard_map/psum | solution.py:151
  11.7 112.8 %copy-start.34 = (f32[384]{0:T(512)}, f32[384]{0:T(512)S(1)}, u32[]{:S(2)}) copy-start(f32[384]{0:T(512)S(1)} %add_rsqrt_fusion.1) | copy-start | bytes 4612
  12.0 115.5 %copy-start.25 = (f32[384,32]{0,1:T(8,128)}, f32[384,32]{0,1:T(8,128)S(1)}, u32[]{:S(2)}) copy-start(f32[384,32]{0,1:T(8,128)S(1)} %get-tuple-element.99) | copy-start | bytes 147460
  12.1 109.2 %copy-start.2 = (bf16[384,2048]{1,0:T(8,128)(2,1)S(1)}, bf16[384,2048]{1,0:T(8,128)(2,1)}, u32[]{:S(2)}) copy-start(bf16[384,2048]{1,0:T(8,128)(2,1)} %param.12) | copy-start | bytes 4718596
  12.1 109.2 %copy-start.31 = (f32[2048]{0:T(1024)S(1)}, f32[2048]{0:T(1024)}, u32[]{:S(2)}) copy-start(f32[2048]{0:T(1024)} %param.14) | copy-start | bytes 24580
  121.3 8.1 copy-start.7
  127.6 1.8 copy-start.10
  127.7 1.8 copy-start.12
  127.7 1.8 copy-start.18
  128.6 2.2 copy-start
  130.8 4.4 copy-start.5
  135.2 1.0 copy-start.27
  135.2 1.0 copy-start.28
  135.2 1.1 copy-start.29
  135.3 286.2 %all-gather.5.cloned.1.call-start = ((), (), s32[]{:S(2)}) async-start(), calls=%async_computation.7 | async-start | bytes 25952256 | tf_op jit(solution)/shard_map/all_gather | solution.py:18
  137.3 393.6 %all-reduce.7.cloned.1.call-start = ((), (), s32[]{:S(2)}) async-start(), calls=%async_computation.8 | async-start | bytes 6291456 | tf_op jit(solution)/shard_map/psum | solution.py:192
  421.5 6.4 copy-start.21
  442.9 7.0 copy-start.36
  442.9 7.0 copy-start.38
  458.5 181.1 %all-reduce.9.cloned.1.call-start = ((), (), s32[]{:S(2)}) async-start(), calls=%async_computation.13 | async-start | bytes 6291456 | tf_op jit(solution)/shard_map/psum | solution.py:163
  530.9 3.4 copy-start.4
  530.9 3.4 copy-start.24
  530.9 3.4 copy-start.30
  535.3 1.7 copy-start.1
  542.2 3.8 copy-start.8
  542.2 3.8 copy-start.9
  542.2 7.7 slice-start
  546.0 9.8 copy-start.20
  546.0 3.9 slice-start.1
  546.0 7.2 slice-start.2
  549.9 1.1 copy-start.11
  549.9 1.1 copy-start.13
  549.9 3.3 slice-start.3
  551.1 1.3 copy-start.19
  551.1 1.8 copy-start.26
  553.2 1.1 copy-start.14
  553.2 1.1 copy-start.16
  558.0 1.0 copy-start.6
  558.1 5.6 copy-start.32
  558.1 5.6 copy-start.35
  558.1 266.7 %reduce-scatter.9.cloned.1.call-start = ((), (), s32[]{:S(2)}) async-start(), calls=%async_computation.9 | async-start | bytes 2162688 | tf_op jit(solution)/shard_map/reduce_scatter | solution.py:258
  563.5 3.1 copy-start.17
  563.6 493.2 %reduce-scatter.13.cloned.1.call-start = ((), (), s32[]{:S(2)}) async-start(), calls=%async_computation.11 | async-start | bytes 6488064
  563.6 3.0 copy-start.3
  566.7 1.4 copy-start.15
  589.6 670.3 %reduce-scatter.11.cloned.1.call-start = ((), (), s32[]{:S(2)}) async-start(), calls=%async_computation.10 | async-start | bytes 8650752 | tf_op jit(solution)/shard_map/reduce_scatter | solution.py:188
  599.5 882.4 %reduce-scatter.15.cloned.1.call-start = ((), (), s32[]{:S(2)}) async-start(), calls=%async_computation.12 | async-start | bytes 17301504
  599.5 6.6 copy-start.22
  599.6 6.6 copy-start.37
  639.5 3.0 copy-start.33
  643.8 23.2 %all-to-all-start = ((f32[32,1,4096]{2,1,0:T(1,128)}), f32[32,1,4096]{2,1,0:T(1,128)}, u32[]{:S(2)}, u32[]{:S(2)}) async-start(f32[32,1,4096]{2,1,0:T(1,128)} %broadcast_in_dim.35), calls=%async_computation | async-start | bytes 1048576 | tf_op jit(solution)/shard_map/all_to_all | solution.py:37
  653.5 5.6 copy-start.23
Sparse Core Ops, SparseCore 0:
  11.7 106.2 all-gather.2
  135.4 72.3 all-reduce.4
  210.8 210.6 all-gather.4
  458.6 72.3 all-reduce.6
  558.2 75.5 all-reduce.8
  636.0 188.6 reduce-scatter.8
  830.7 226.0 reduce-scatter.12
  1059.3 200.5 reduce-scatter.10
  1262.4 219.4 reduce-scatter.14
where the time goes:
time: 1500 us; the launch traced here: 1490 us
  waiting for transfers between devices  1260 us (84%)
  matrix products  110 us (7%)
  other arithmetic  51.5 us (3%)
  local copies, waits for them, and re-layouts  44.7 us (3%)
    unnamed x11, waiting for transfers between devices  451 us
    all_gather x2, waiting for transfers between devices, turned_gather(): result = lax.all_gather(both, axis, axis=0, tiled=True)  315 us
    reduce_scatter x1, waiting for transfers between devices, per_device(): lax.psum_scatter(down_term.astype(jnp.bfloat16), 'dp', scatter_dimension=...  200 us
    reduce_scatter x1, waiting for transfers between devices, per_device(): lax.psum_scatter(output_term.astype(jnp.bfloat16), 'dp', scatter_dimensio...  156 us
    psum x1, waiting for transfers between devices, per_device(): branch = lax.psum(local_dot(attended, output_full), 'tensor')  70.2 us
    psum x1, waiting for transfers between devices, per_device(): normed_two_grad = lax.psum(feed_input, 'tensor')  63.6 us
    unnamed x98, local copies, waits for them, and re-layouts  38.8 us
    dot_general x7, matrix products, local_dot(): return jnp.dot(left, right, preferred_element_type=jnp.float32)  37.1 us
  transfers between devices with their start and end apart: 10, of which 9 were waited for; matrix products, arithmetic and copies ran while one was open for 8% of the time, Pallas kernels for 0%

commit v1 on v0

v1 whole, which is shorter than its diff:
```python
import functools

import jax
import jax.numpy as jnp
from jax import lax
from jax.experimental import pallas as pl
from jax.experimental.pallas import tpu as pltpu
from jax.sharding import Mesh, PartitionSpec as P

HEAD = 64
MIB = 1024 * 1024

norm_epsilon = 1e-05
rope_base = 130000.0
masked_score = -1000000000.0

AXES = ("y", "xh", "z", "xl", "c")
SIZES = (4, 2, 4, 2, 2)
DP = ("y", "xh", "z")
TP = ("xl", "c")

f32 = jnp.float32
bf16 = jnp.bfloat16


def swap(axis, mask, size):
    perm = [(i, i ^ mask) for i in range(size)]
    return lambda value: lax.ppermute(value, axis, perm)


core = swap("c", 1, 2)
y_ring = (swap("y", 1, 4), swap("y", 3, 4), swap("y", 2, 4))
z_ring = (swap("z", 1, 4), swap("z", 3, 4), swap("z", 2, 4))
x_ring = (swap(("xh", "xl"), 1, 4), swap(("xh", "xl"), 3, 4), swap(("xh", "xl"), 2, 4))


def ring_first(parts, ring):
    return ring[0](parts[2]), ring[1](parts[3])


def ring_between(parts, arrived):
    half = parts[2].shape[0]
    to_third, to_first = arrived
    first = jnp.concatenate([parts[1][:half], parts[1][half:] + to_first], axis=0)
    third = jnp.concatenate([parts[4][:half] + to_third, parts[4][half:]], axis=0)
    return first, third


def both_ways(values, ring):
    return ring[0](values[0]), ring[1](values[1])


def line_gather(own):
    sides = both_ways((own, own), x_ring)
    mine = stacked(ring_pieces(own, sides, opposite_halves(sides, x_ring)))
    return stacked([mine, core(mine)])


def opposite_halves(arrived, ring):
    first, third = arrived
    half = first.shape[0] // 2
    return ring[0](third[:half]), ring[1](first[half:])


def ring_pieces(own, arrived, halves):
    return [own, arrived[0], *halves, arrived[1]]


def direct(value, ring):
    near, far, opposite = ring
    return near(value), opposite(value), far(value)


def sum_round(value, arrived):
    near, opposite, far = arrived
    return (value + near) + (opposite + far)


def total(terms):
    result = terms[0].astype(f32)
    for term in terms[1:]:
        result = result + term.astype(f32)
    return result


def sum_split_kernel(terms, *refs):
    row = 0
    for out in refs[terms:]:
        rows = out.shape[0]
        value = refs[0][row : row + rows, :].astype(f32)
        for ref in refs[1:terms]:
            value = value + ref[row : row + rows, :].astype(f32)
        out[...] = value.astype(out.dtype)
        row += rows


def sum_split(terms, cuts):
    width = terms[0].shape[1]
    whole = pl.BlockSpec(memory_space=pltpu.VMEM)
    rows = sum(cuts)
    return pl.pallas_call(
        functools.partial(sum_split_kernel, len(terms)),
        out_shape=[jax.ShapeDtypeStruct((cut, width), bf16) for cut in cuts],
        in_specs=[whole] * len(terms),
        out_specs=[whole] * len(cuts),
        cost_estimate=pl.CostEstimate(
            flops=rows * width * len(terms),
            bytes_accessed=rows * width * 2 * (len(terms) + 1),
            transcendentals=0,
        ),
        compiler_params=pltpu.CompilerParams(vmem_limit_bytes=2 * rows * width * 2 * (len(terms) + 1) + 4 * MIB),
        name="sum_split",
    )(*terms)


def ring_cuts(rows):
    quarter = rows // 4
    return (quarter, quarter, quarter // 2, quarter // 2, quarter)


def pack_kernel(moves, count, offsets, *refs):
    sems = refs[-1]

    def at(row):
        return row if isinstance(row, int) else pl.multiple_of(offsets[row[0]], 16)

    copies = []
    for k, (i, start, rows, out, to, column, columns) in enumerate(moves):
        copies.append(
            pltpu.make_async_copy(
                refs[i].at[pl.ds(at(start), rows), pl.ds(column, columns)],
                refs[count + out].at[pl.ds(at(to), rows), :],
                sems.at[k],
            )
        )
    for copy in copies:
        copy.start()
    for copy in copies:
        copy.wait()


def pack(pieces, moves, offsets, shapes):
    anywhere = pl.BlockSpec(memory_space=pl.ANY)
    total = 2 * sum(2 * r * c for r, c in shapes)
    return pl.pallas_call(
        functools.partial(pack_kernel, tuple(moves), len(pieces)),
        out_shape=[jax.ShapeDtypeStruct(shape, pieces[0].dtype) for shape in shapes],
        in_specs=[pl.BlockSpec(memory_space=pltpu.SMEM)] + [anywhere] * len(pieces),
        out_specs=[pl.BlockSpec(memory_space=pltpu.VMEM)] * len(shapes),
        scratch_shapes=[pltpu.SemaphoreType.DMA((len(moves),))],
        compiler_params=pltpu.CompilerParams(vmem_limit_bytes=total + 2 * MIB),
        cost_estimate=pl.CostEstimate(flops=0, bytes_accessed=total, transcendentals=0),
        name="pack",
    )(offsets, *pieces)


def stacked(pieces):
    moves, row = [], 0
    for i, p in enumerate(pieces):
        moves.append((i, 0, p.shape[0], 0, row, 0, p.shape[1]))
        row += p.shape[0]
    offsets = jnp.zeros((1,), jnp.int32)
    return pack(pieces, moves, offsets, [(row, pieces[0].shape[1])])[0]


def choose_kernel(moves, count, *refs):
    sems = refs[-1]
    xh = lax.axis_index("xh")
    which = (xh, 1 - xh)
    copies = []
    for k, (i, half, start, width, to) in enumerate(moves):
        for out in range(2):
            at = pl.multiple_of(which[out] * half + start, 128)
            copies.append(
                pltpu.make_async_copy(
                    refs[i].at[:, pl.ds(at, width)],
                    refs[count + out].at[:, pl.ds(to, width)],
                    sems.at[2 * k + out],
                )
            )
    for copy in copies:
        copy.start()
    for copy in copies:
        copy.wait()


def own_columns(blocks, tiles):
    moves, to = [], 0
    for k, start, width in tiles:
        moves.append((k, blocks[k].shape[1] // 2, start, width, to))
        to += width
    rows = blocks[0].shape[0]
    anywhere = pl.BlockSpec(memory_space=pl.ANY)
    return pl.pallas_call(
        functools.partial(choose_kernel, tuple(moves), len(blocks)),
        out_shape=[jax.ShapeDtypeStruct((rows, to), bf16)] * 2,
        in_specs=[anywhere] * len(blocks),
        out_specs=[pl.BlockSpec(memory_space=pltpu.VMEM)] * 2,
        scratch_shapes=[pltpu.SemaphoreType.DMA((2 * len(moves),))],
        compiler_params=pltpu.CompilerParams(vmem_limit_bytes=56 * MIB),
        cost_estimate=pl.CostEstimate(flops=0, bytes_accessed=8 * rows * to, transcendentals=0),
        name="choose",
    )(*blocks)


def gather_weights(sent, xh):
    own = jnp.concatenate(to_columns(*both_ways(sent, x_ring), xh), axis=0)
    return lax.all_gather(own, ("y", "z"), axis=0, tiled=True)


def to_columns(first, second, xh):
    return jnp.where(xh == 0, first, second), jnp.where(xh == 0, second, first)


def deliver_kernel(moves, which, same_ref, other_ref, *outs):
    mine = which[0] == 0
    for out, start, width, at in moves:
        same, other = same_ref[:, start : start + width], other_ref[:, start : start + width]
        half = outs[out].shape[1] // 2
        outs[out][:, at : at + width] = jnp.where(mine, same, other).astype(f32)
        outs[out][:, half + at : half + at + width] = jnp.where(mine, other, same).astype(f32)


def delivered(same, other, xh, tiles, widths):
    moves, start = [], 0
    for out, at, width in tiles:
        moves.append((out, start, width, at))
        start += width
    whole = pl.BlockSpec(memory_space=pltpu.VMEM)
    rows = same.shape[0]
    return pl.pallas_call(
        functools.partial(deliver_kernel, tuple(moves)),
        out_shape=[jax.ShapeDtypeStruct((rows, width), f32) for width in widths],
        in_specs=[pl.BlockSpec(memory_space=pltpu.SMEM), whole, whole],
        out_specs=[whole] * len(widths),
        cost_estimate=pl.CostEstimate(
            flops=0, bytes_accessed=12 * rows * start, transcendentals=0
        ),
        compiler_params=pltpu.CompilerParams(vmem_limit_bytes=12 * MIB),
        name="delivered",
    )(jnp.stack([xh]).astype(jnp.int32), same, other)


def by_tensor(pieces, moves, rows, xl, c, count=1):
    width = pieces[0].shape[1] // count
    offsets = jnp.stack([((xl ^ m[2]) * 2 + (c ^ m[3])) * rows for m in moves]).astype(jnp.int32)
    moves = [
        (m[0], m[1], rows, out, (k,), out * width, width)
        for k, m in enumerate(moves)
        for out in range(count)
    ]
    return pack(pieces, moves, offsets, [(4 * rows, width)] * count)


def line_offsets(rows, xl, c):
    places = [((xl ^ r_xl) * 2 + (c ^ r_c)) * rows for r_c in range(2) for r_xl in range(2)]
    return jnp.stack(places).astype(jnp.int32)


def for_the_line(value, rows, offsets):
    width = value.shape[1]
    moves = [(0, (1 - k,), rows, 0, k * rows, 0, width) for k in range(2)]
    return pack([value], moves, offsets, [(2 * rows, width)])[0]


def of_the_line(value, other, rows, offsets):
    width = value.shape[1]
    moves = []
    for r_c in range(2):
        to = 4 * r_c * rows
        moves += [(0, (2 * r_c + k,), rows, 0, to + k * rows, 0, width) for k in range(2)]
        moves.append((1 + r_c, 0, 2 * rows, 0, to + 2 * rows, 0, width))
    return pack([value, other, core(other)], moves, offsets, [(8 * rows, width)])[0]


def layout(lengths, places):
    ends = jnp.cumsum(lengths)
    passed = places[:, None] >= ends[None, :]
    segment = jnp.sum(passed.astype(jnp.int32), axis=1)
    begins = jnp.max(jnp.where(passed, ends[None, :], jnp.zeros_like(ends)[None, :]), axis=1)
    return (segment, places - begins)


def rotary(position):
    lane = jnp.arange(2 * HEAD, dtype=jnp.int32)
    index = (lane % (HEAD // 2)).astype(f32)
    frequency = rope_base ** (-2.0 * index / HEAD)
    angle = position.astype(f32)[:, None] * frequency[None, :]
    sign = jnp.where(lane % HEAD < HEAD // 2, -1.0, 1.0).astype(f32)
    return (jnp.cos(angle), jnp.sin(angle) * sign[None, :])


def other_half(values):
    width = values.shape[1]
    half = HEAD // 2
    lane = lax.broadcasted_iota(jnp.int32, values.shape, 1)
    up, down = pltpu.roll(values, width - half, 1), pltpu.roll(values, half, 1)
    return jnp.where(lane % HEAD < half, up, down)


def widened(table, width):
    return jnp.concatenate([table] * (width // table.shape[1]), axis=1)


def attend_kernel(qkv_ref, cos_ref, sin_ref, mask_ref, rot_ref, out_ref, lse_ref):
    _, _, part, width = qkv_ref.shape
    rows, width = 2 * part, width // 3

    def columns(ref, start, size):
        return ref[:, :, :, start : start + size].reshape(rows, size)

    cosine = widened(columns(cos_ref, 0, cos_ref.shape[3]), width)
    sine = widened(columns(sin_ref, 0, sin_ref.shape[3]), width)
    query = columns(qkv_ref, 0, width)
    query = ((query * cosine + other_half(query) * sine) * HEAD ** (-0.5)).astype(bf16)
    key = columns(qkv_ref, width, width)
    key = (key * cosine + other_half(key) * sine).astype(bf16)
    value = columns(qkv_ref, 2 * width, width).astype(bf16)
    for i, low in enumerate((query, key, value)):
        rot_ref[:, :, :, i * width : (i + 1) * width] = low.reshape(2, 1, part, width)
    value_t = value.astype(f32).T.astype(bf16)
    allowed = mask_ref[0] > 0.0
    lane = lax.broadcasted_iota(jnp.int32, query.shape, 1) // HEAD
    outs = []
    for head in range(width // HEAD):
        one = jnp.where(lane == head, query, jnp.zeros_like(query))
        scores = jnp.where(allowed, dot_right_t(key, one), masked_score)
        top = jnp.max(scores, axis=0, keepdims=True)
        total = top + jnp.log(jnp.sum(jnp.exp(scores - top), axis=0, keepdims=True))
        probs = jnp.exp(scores - total).astype(bf16)
        lse_ref[0, head : head + 1, :] = total
        outs.append(local_dot(value_t[head * HEAD : (head + 1) * HEAD], probs))
    out = jnp.concatenate(outs, axis=0).T
    out_ref[...] = out.astype(bf16).reshape(2, 1, part, width)


def attend_back_kernel(
    rot_ref, grad_ref, lse_ref, cos_ref, sin_ref, mask_ref, out_ref, dv_ref, dk_ref, dq_ref
):
    _, _, part, width = grad_ref.shape
    rows = 2 * part

    def columns(ref, start, size):
        return ref[:, :, :, start : start + size].reshape(rows, size)

    query, key, value = (columns(rot_ref, i * width, width) for i in range(3))
    grad = columns(grad_ref, 0, width)
    key_t = key.astype(f32).T.astype(bf16)
    allowed = mask_ref[0] > 0.0
    lane = lax.broadcasted_iota(jnp.int32, query.shape, 1) // HEAD
    for head in range(width // HEAD):
        one = jnp.where(lane == head, query, jnp.zeros_like(query))
        one_grad = jnp.where(lane == head, grad, jnp.zeros_like(grad))
        scores = jnp.where(allowed, dot_right_t(key, one), masked_score)
        probs = jnp.exp(scores - lse_ref[0, head : head + 1, :])
        prob_grad = dot_right_t(value, one_grad)
        shift = jnp.sum(probs * prob_grad, axis=0, keepdims=True)
        score_grad = (probs * (prob_grad - shift)).astype(bf16)
        dv = local_dot(probs.astype(bf16), one_grad)
        dk = local_dot(score_grad, one)
        if head == 0:
            dv_ref[...] = dv
            dk_ref[...] = dk
        else:
            dv_ref[...] += dv
            dk_ref[...] += dk
        dq_ref[head * HEAD : (head + 1) * HEAD, :] = local_dot(
            key_t[head * HEAD : (head + 1) * HEAD], score_grad
        )
    cosine = widened(columns(cos_ref, 0, cos_ref.shape[3]), width)
    sine = widened(columns(sin_ref, 0, sin_ref.shape[3]), width)
    dq = dq_ref[...].T * HEAD ** (-0.5)
    dq = dq * cosine - other_half(dq) * sine
    dk = dk_ref[...]
    dk = dk * cosine - other_half(dk) * sine
    for i, term in enumerate((dq, dk, dv_ref[...])):
        out_ref[:, :, :, i * width : (i + 1) * width] = term.astype(bf16).reshape(
            2, 1, part, width
        )


def by_block(columns, part):
    return pl.BlockSpec((2, 1, part, columns), lambda i: (0, i, 0, 0))


def attend(qkv, cosine, sine, mask):
    rows, width = qkv.shape
    part, width = rows // 4, width // 3
    heads = width // HEAD
    table = cosine.shape[1]
    rot, out, lse = pl.pallas_call(
        attend_kernel,
        grid=(2,),
        in_specs=[
            by_block(3 * width, part),
            by_block(table, part),
            by_block(table, part),
            pl.BlockSpec((1, 2 * part, 2 * part), lambda i: (i, 0, 0)),
        ],
        out_specs=[
            by_block(3 * width, part),
            by_block(width, part),
            pl.BlockSpec((1, heads, 2 * part), lambda i: (i, 0, 0)),
        ],
        out_shape=[
            jax.ShapeDtypeStruct((2, 2, part, 3 * width), bf16),
            jax.ShapeDtypeStruct((2, 2, part, width), bf16),
            jax.ShapeDtypeStruct((2, heads, 2 * part), f32),
        ],
        cost_estimate=pl.CostEstimate(
            flops=2 * 2 * heads * (2 * part) ** 2 * (width + HEAD),
            bytes_accessed=rows * width * 30,
            transcendentals=2 * 2 * heads * (2 * part) ** 2,
        ),
        compiler_params=pltpu.CompilerParams(vmem_limit_bytes=24 * MIB),
        name="attend",
    )(
        qkv.reshape(2, 2, part, 3 * width),
        cosine.reshape(2, 2, part, table),
        sine.reshape(2, 2, part, table),
        mask,
    )
    return rot, out.reshape(rows, width), lse


def attend_back(rot, grad, lse, cosine, sine, mask):
    rows, width = grad.shape
    part, heads, table = rows // 4, width // HEAD, cosine.shape[1]
    out = pl.pallas_call(
        attend_back_kernel,
        grid=(2,),
        in_specs=[
            by_block(3 * width, part),
            by_block(width, part),
            pl.BlockSpec((1, heads, 2 * part), lambda i: (i, 0, 0)),
            by_block(table, part),
            by_block(table, part),
            pl.BlockSpec((1, 2 * part, 2 * part), lambda i: (i, 0, 0)),
        ],
        out_specs=by_block(3 * width, part),
        out_shape=jax.ShapeDtypeStruct((2, 2, part, 3 * width), bf16),
        scratch_shapes=[
            pltpu.VMEM((2 * part, width), f32),
            pltpu.VMEM((2 * part, width), f32),
            pltpu.VMEM((width, 2 * part), f32),
        ],
        cost_estimate=pl.CostEstimate(
            flops=2 * 2 * heads * (2 * part) ** 2 * (4 * width + HEAD),
            bytes_accessed=rows * width * 30,
            transcendentals=2 * heads * (2 * part) ** 2,
        ),
        compiler_params=pltpu.CompilerParams(vmem_limit_bytes=24 * MIB),
        name="attend_back",
    )(
        rot,
        grad.reshape(2, 2, part, width),
        lse,
        cosine.reshape(2, 2, part, table),
        sine.reshape(2, 2, part, table),
        mask,
    )
    return out.reshape(rows, 3 * width)


def local_dot(left, right):
    return jnp.dot(left, right, preferred_element_type=f32)


def dot_right_t(left, right):
    return lax.dot_general(left, right, (((1,), (1,)), ((), ())), preferred_element_type=f32)


def dot_left_t(left, right):
    return lax.dot_general(left, right, (((0,), (0,)), ((), ())), preferred_element_type=f32)


def transpose_kernel(value_ref, out_ref):
    out_ref[...] = value_ref[...].T


def transposed(value):
    rows, width = value.shape
    tile = width // 4
    return pl.pallas_call(
        transpose_kernel,
        grid=(4,),
        in_specs=[pl.BlockSpec((rows, tile), lambda i: (0, i))],
        out_specs=pl.BlockSpec((tile, rows), lambda i: (i, 0)),
        out_shape=jax.ShapeDtypeStruct((width, rows), value.dtype),
        cost_estimate=pl.CostEstimate(
            flops=0, bytes_accessed=4 * rows * width, transcendentals=0
        ),
        compiler_params=pltpu.CompilerParams(vmem_limit_bytes=8 * MIB),
        name="transposed",
    )(value)


def weight_grads_kernel(steps, left_ref, right_ref, *refs):
    out = refs[-1]
    columns = right_ref[...]
    tall = out.shape[0] // steps
    for start in range(0, out.shape[0], tall):
        out[start : start + tall, :] = local_dot(
            left_ref[start : start + tall, :], columns
        ).astype(bf16)


def weight_grads(left, right, tile, steps, columns, first, into=()):
    width, tokens = left.shape
    count = right.shape[1]
    anywhere = pl.BlockSpec(memory_space=pl.ANY)
    to = first // tile
    return pl.pallas_call(
        functools.partial(weight_grads_kernel, steps),
        grid=(count // tile,),
        in_specs=[
            pl.BlockSpec(memory_space=pltpu.VMEM),
            pl.BlockSpec((tokens, tile), lambda i: (0, i)),
        ]
        + [anywhere] * len(into),
        out_specs=pl.BlockSpec((width, tile), lambda i: (0, to + i)),
        out_shape=jax.ShapeDtypeStruct((width, columns), bf16),
        input_output_aliases={2 + k: k for k in range(len(into))},
        cost_estimate=pl.CostEstimate(
            flops=2 * tokens * width * count,
            bytes_accessed=2 * (tokens * width + (tokens + width) * count),
            transcendentals=0,
        ),
        compiler_params=pltpu.CompilerParams(vmem_limit_bytes=44 * MIB),
        name="weight_grads",
    )(left, right, *into)


def feed_kernel(normed_ref, cot_ref, gate_up_ref, down_ref, mixed_ref, grad_ref):
    units = mixed_ref.shape[1]
    gate_up = local_dot(normed_ref[...], gate_up_ref[...])
    gate, up = gate_up[:, :units], gate_up[:, units:]
    back = local_dot(cot_ref[...], down_ref[...])
    sigmoid = jax.nn.sigmoid(gate)
    silu = gate * sigmoid
    mixed_ref[...] = (silu * up).astype(bf16)
    grad_ref[:, :units] = (back * up * sigmoid * (1.0 + gate * (1.0 - sigmoid))).astype(bf16)
    grad_ref[:, units:] = (back * silu).astype(bf16)


def feed(normed, cot, full, units, tile):
    rows, width = normed.shape
    steps = units // tile
    return pl.pallas_call(
        feed_kernel,
        grid=(steps,),
        in_specs=[
            pl.BlockSpec((rows, width), lambda i: (0, 0)),
            pl.BlockSpec((rows, width), lambda i: (0, 0)),
            pl.BlockSpec((width, 2 * tile), lambda i: (0, i)),
            pl.BlockSpec((width, tile), lambda i: (0, 2 * steps + i)),
        ],
        out_specs=[
            pl.BlockSpec((rows, tile), lambda i: (0, i)),
            pl.BlockSpec((rows, 2 * tile), lambda i: (0, i)),
        ],
        out_shape=[
            jax.ShapeDtypeStruct((rows, units), bf16),
            jax.ShapeDtypeStruct((rows, 2 * units), bf16),
        ],
        cost_estimate=pl.CostEstimate(
            flops=6 * rows * width * units,
            bytes_accessed=2 * (2 * rows * width + 3 * (rows + width) * units),
            transcendentals=rows * units,
        ),
        compiler_params=pltpu.CompilerParams(vmem_limit_bytes=52 * MIB),
        name="feed",
    )(normed, cot, full, full)


def to_width_kernel(left_ref, full_ref, *refs):
    low_ref, high_ref = refs[-2:]
    rows = low_ref.shape[0]
    high_ref[...] = dot_right_t(left_ref[rows:, :], full_ref[...]).astype(bf16)
    low_ref[...] = dot_right_t(left_ref[:rows, :], full_ref[...]).astype(bf16)


def to_width(left, full, at, columns, first, into=()):
    rows, depth, width = left.shape[0] // 2, left.shape[1], full.shape[0]
    tile = width // 4
    to = first // tile
    anywhere = pl.BlockSpec(memory_space=pl.ANY)
    return pl.pallas_call(
        to_width_kernel,
        grid=(4,),
        in_specs=[
            pl.BlockSpec(memory_space=pltpu.VMEM),
            pl.BlockSpec((tile, depth), lambda i: (i, at)),
        ]
        + [anywhere] * len(into),
        out_specs=[pl.BlockSpec((rows, tile), lambda i: (0, to + i))] * 2,
        out_shape=[jax.ShapeDtypeStruct((rows, columns), bf16)] * 2,
        input_output_aliases={2 + k: k for k in range(len(into))},
        cost_estimate=pl.CostEstimate(
            flops=4 * rows * depth * width,
            bytes_accessed=2 * (2 * rows * depth + width * (2 * rows + depth)),
            transcendentals=0,
        ),
        compiler_params=pltpu.CompilerParams(vmem_limit_bytes=44 * MIB),
        name="to_width",
    )(left, full, *into)


INWARD = [(g // 8 * 2 + g % 2) * 4 + g // 2 % 4 for g in range(32)]
OUTWARD = [(n // 8 * 4 + n % 4) * 2 + n // 4 % 2 for n in range(32)]
BOTH_OUTWARD = OUTWARD + [32 + g for g in OUTWARD]


def middle_kernel(hidden_ref, own_ref, near_ref, far_ref, gain_ref, middle_ref, normed_ref):
    middle = hidden_ref[...].astype(f32) + own_ref[...].astype(f32)
    middle = middle + near_ref[...].astype(f32) + far_ref[...].astype(f32)
    scale = lax.rsqrt(jnp.mean(middle * middle, axis=-1, keepdims=True) + norm_epsilon)
    middle_ref[...] = middle
    normed_ref[...] = (middle * scale * gain_ref[...]).astype(bf16)


def middle_norm(hidden, terms, gain):
    whole = pl.BlockSpec(memory_space=pltpu.VMEM)
    return pl.pallas_call(
        middle_kernel,
        out_shape=[
            jax.ShapeDtypeStruct(hidden.shape, f32),
            jax.ShapeDtypeStruct(hidden.shape, bf16),
        ],
        in_specs=[whole] * 5,
        out_specs=[whole] * 2,
        compiler_params=pltpu.CompilerParams(vmem_limit_bytes=12 * MIB),
        name="middle_norm",
    )(hidden, *terms, gain)


def turn_kernel(groups, value_ref, out_ref):
    value = value_ref[...].astype(f32)
    chunk = value.shape[1] // len(groups)
    parts = [value[:, g * chunk : (g + 1) * chunk] for g in groups]
    out_ref[...] = jnp.concatenate(parts, axis=1).astype(bf16)


def turned(value, groups):
    whole = pl.BlockSpec(memory_space=pltpu.VMEM)
    return pl.pallas_call(
        functools.partial(turn_kernel, tuple(groups)),
        out_shape=jax.ShapeDtypeStruct(value.shape, bf16),
        in_specs=[whole],
        out_specs=whole,
        compiler_params=pltpu.CompilerParams(vmem_limit_bytes=16 * MIB),
        name="turned",
    )(value)


def inward(gain):
    return jnp.swapaxes(gain.reshape(4, 2, 4, -1), 1, 2).reshape(1, -1)


def outward(gains):
    return jnp.swapaxes(gains.reshape(2, 4, 4, 2, -1), 2, 3).reshape(2, -1)


def per_device(
    tokens,
    seq_lengths,
    attention_gain,
    feedforward_gain,
    query_weight,
    key_weight,
    value_weight,
    output_weight,
    gate_weight,
    up_weight,
    down_weight,
    cotangent,
):
    y, xh, z, xl, c = (lax.axis_index(a) for a in AXES)
    block, width = tokens.shape
    rows = block // 4
    chunk = width // 32
    pair, cross = x_ring[:2]
    stage = lax.optimization_barrier

    third = query_weight.shape[1] // 2
    units = gate_weight.shape[1] // 2
    tile = units // 4
    gain_one, gain_two = inward(attention_gain), inward(feedforward_gain)

    attention_tiles = [(k, 0, third) for k in range(4)]
    feed_tiles = [(k, j * tile, tile) for j in range(4) for k in range(2)] + [(2, 0, units)]
    sent = own_columns(
        (query_weight, key_weight, value_weight, output_weight.T),
        attention_tiles,
    )
    feed_blocks = (gate_weight, up_weight, down_weight.T)
    sent, feed_blocks, tokens, cotangent = stage((sent, feed_blocks, tokens, cotangent))
    attention_full = gather_weights(sent, xh)
    feed_full = gather_weights(own_columns(feed_blocks, feed_tiles), xh)
    offsets = line_offsets(rows, xl, c)
    tokens_in, cotangent_in = turned(tokens, INWARD), turned(cotangent, INWARD)
    other = cross(for_the_line(tokens_in, rows, offsets))
    sent = for_the_line(cotangent_in, rows, offsets)
    other, sent = stage((other, sent))
    cot_other = cross(sent)
    hidden_low = of_the_line(tokens_in, other, rows, offsets)
    x_own = hidden_low[:rows]

    lengths = jnp.stack([seq_lengths, cross(seq_lengths)])
    step = jnp.arange(block, dtype=jnp.int32)
    at_c, at_xl, at_row = step // (2 * rows), (step // rows) % 2, step % rows
    block_rows = ((xl ^ at_xl) * 2 + (c ^ at_c)) * rows + at_row
    segment, position = jax.vmap(layout, (0, None))(lengths, block_rows)
    mask = (segment[:, :, None] == segment[:, None, :]) & (
        block_rows[:, None] <= block_rows[None, :]
    )
    mask = mask.astype(f32)
    by_row = jnp.swapaxes(position.reshape(2, 2, block // 2), 0, 1).reshape(2 * block)
    cosine, sine = rotary(by_row)

    hidden = hidden_low.astype(f32)
    scale_one = lax.rsqrt(jnp.mean(hidden * hidden, axis=-1, keepdims=True) + norm_epsilon)
    normed_one = (hidden * scale_one * gain_one).astype(bf16)
    normed_one, mask, cosine, sine, cot_other = stage((normed_one, mask, cosine, sine, cot_other))
    cot = of_the_line(cotangent_in, cot_other, rows, offsets)
    c_own = cot[:rows]
    qkv_full, out_full = pack(
        [attention_full],
        [(0, 0, width, 0, 0, 0, 3 * third), (0, 0, width, 1, 0, 3 * third, third)],
        jnp.zeros((1,), jnp.int32),
        [(width, 3 * third), (width, third)],
    )
    qkv = local_dot(normed_one, qkv_full)
    rot, attended, lse = attend(qkv, cosine, sine, mask)
    from_core = core(dot_right_t(attended[block:], out_full).astype(bf16))
    parts = sum_split(
        [dot_right_t(attended[:block], out_full).astype(bf16), from_core], ring_cuts(block)
    )
    sides = ring_between(parts, ring_first(parts, x_ring))
    middle, n2_own = middle_norm(x_own, (parts[0], *both_ways(sides, x_ring)), gain_two)
    n2_sides = both_ways((n2_own, n2_own), x_ring)
    n1_turned, cot_turned = transposed(normed_one), transposed(cot)
    n2_sides, n1_turned, cot_turned = stage((n2_sides, n1_turned, cot_turned))
    n2_mine = stacked(ring_pieces(n2_own, n2_sides, opposite_halves(n2_sides, x_ring)))
    normed_two = stacked([n2_mine, core(n2_mine)])
    normed_two, n2_turned = stage((normed_two, transposed(normed_two)))

    mixed_low, gate_up_grad = feed(normed_two, cot, feed_full, units, tile)
    wide = units // 2
    gate_up_term = weight_grads(n2_turned, gate_up_grad, units // 2, 4, 2 * units, 0)
    gate_up_grad, gate_up_term, mixed_low = stage((gate_up_grad, gate_up_term, mixed_low))
    gate_up_sum = lax.psum_scatter(gate_up_term, ("y", "z"), scatter_dimension=0, tiled=True)
    mine, high = to_width(gate_up_grad, feed_full, 0, width, 0)
    mine, high, mixed_low = stage((mine, high, mixed_low))
    from_core = core(high)
    rest_term = weight_grads(cot_turned, mixed_low, units // 2, 4, units + 4 * third, 0)
    from_core, rest_term = stage((from_core, rest_term))
    parts = sum_split([mine, from_core], ring_cuts(block))
    arrived, mixed_low = stage((ring_first(parts, x_ring), mixed_low))
    sides = both_ways(ring_between(parts, arrived), x_ring)
    both = to_width(mixed_low, feed_full, 2, 2 * width, 0)
    sides, both = stage((sides, both))
    normed_two_grad = total([parts[0], *sides])
    scale_two = lax.rsqrt(jnp.mean(middle * middle, axis=-1, keepdims=True) + norm_epsilon)
    middle_unit = middle * scale_two
    weighted_two = normed_two_grad * gain_two
    middle_grad = c_own.astype(f32) + scale_two * (
        weighted_two - middle_unit * jnp.mean(weighted_two * middle_unit, axis=-1, keepdims=True)
    )
    gain_two_part = jnp.sum(normed_two_grad * middle_unit, axis=0, keepdims=True)
    middle_grad_low = line_gather(middle_grad.astype(bf16))

    attended_grad = local_dot(middle_grad_low, out_full).astype(bf16)
    qkv_grad = attend_back(rot, attended_grad, lse, cosine, sine, mask)
    rest_term = weight_grads(
        transposed(middle_grad_low),
        attended,
        third,
        4,
        units + 4 * third,
        units + 3 * third,
        (rest_term,),
    )
    rest_term = weight_grads(
        n1_turned, qkv_grad, third, 4, units + 4 * third, units, (rest_term,)
    )
    qkv_grad, rest_term = stage((qkv_grad, rest_term))
    rest_term, gate_up_sum = stage((rest_term, gate_up_sum))
    rest_sum = lax.psum_scatter(rest_term, ("y", "z"), scatter_dimension=0, tiled=True)

    mine, high = to_width(qkv_grad, qkv_full, 0, 2 * width, width, tuple(both))
    from_core = core(high)
    gain_one_part = jnp.sum(
        jnp.concatenate([mine[:, width:], high[:, width:]], axis=0).astype(f32)
        * (hidden * scale_one),
        axis=0,
        keepdims=True,
    )
    gains = jnp.concatenate([gain_one_part, gain_two_part], axis=0)
    gains_core = core(gains)
    parts = sum_split([mine, from_core], ring_cuts(block))
    arrived = ring_first(parts, x_ring)
    arrived, gains_core = stage((arrived, gains_core))

    sides = both_ways(ring_between(parts, arrived), x_ring)
    gains = gains + gains_core
    gains_ways = direct(gains, x_ring)
    (middle_back,) = by_tensor(
        [middle_grad_low], [(0, k * rows, k % 2, k // 4) for k in (0, 1, 4, 5)], rows, xl, c
    )
    middle_back = turned(middle_back, OUTWARD)
    sides, gains_ways, middle_back = stage((sides, gains_ways, middle_back))

    sums = total([parts[0], *sides])
    both_own = jnp.concatenate([middle + sums[:, :width], sums[:, width:]], axis=1)
    both_own = turned(both_own.astype(bf16), BOTH_OUTWARD)
    both_pair = pair(both_own)
    gains = sum_round(gains, gains_ways)
    gains_ways = direct(gains, y_ring)
    both_pair, gains_ways = stage((both_pair, gains_ways))

    both_core = core(stacked([both_own, both_pair]))
    gains = sum_round(gains, gains_ways)
    gains_ways = direct(gains, z_ring)
    feed_own = both_ways(to_columns(gate_up_sum[:chunk], gate_up_sum[chunk:], xh), x_ring)
    gains_ways, both_core, feed_own = stage((gains_ways, both_core, feed_own))

    gains = outward(sum_round(gains, gains_ways))
    layer_out, normed_one_grad = by_tensor(
        [both_own, both_pair, both_core],
        [(0, 0, 0, 0), (1, 0, 1, 0), (2, 0, 0, 1), (2, rows, 1, 1)],
        rows,
        xl,
        c,
        2,
    )
    normed_one_grad = normed_one_grad.astype(f32)
    gate_grad, up_grad = delivered(*feed_own, xh, feed_tiles[:-1], (2 * units,) * 2)
    own = tokens.astype(f32)
    own_scale = lax.rsqrt(jnp.mean(own * own, axis=-1, keepdims=True) + norm_epsilon)
    own_unit = own * own_scale
    weighted_one = normed_one_grad * attention_gain
    tokens_grad = middle_back.astype(f32) + own_scale * (
        weighted_one - own_unit * jnp.mean(weighted_one * own_unit, axis=-1, keepdims=True)
    )
    (tokens_grad, gains, gate_grad, up_grad, rest_sum) = stage(
        (tokens_grad, gains, gate_grad, up_grad, rest_sum)
    )
    rest_own = both_ways(to_columns(rest_sum[:chunk], rest_sum[chunk:], xh), x_ring)
    down_grad, query_grad, key_grad, value_grad, output_grad = delivered(
        *rest_own,
        xh,
        [(0, 0, units)] + [(k + 1, 0, third) for k in range(4)],
        (2 * units,) + (2 * third,) * 4,
    )
    return (
        layer_out,
        tokens_grad,
        gains[0],
        gains[1],
        query_grad,
        key_grad,
        value_grad,
        output_grad.T,
        gate_grad,
        up_grad,
        down_grad.T,
    )


def solution(mesh):
    named = Mesh(mesh.devices.reshape(SIZES), AXES)
    return jax.shard_map(
        per_device,
        mesh=named,
        in_specs=(
            P(DP, None),
            P(DP),
            P(),
            P(),
            P(DP, TP),
            P(DP, TP),
            P(DP, TP),
            P(TP, DP),
            P(DP, TP),
            P(DP, TP),
            P(TP, DP),
            P(DP, None),
        ),
        out_specs=(
            P(DP, None),
            P(DP, None),
            P(),
            P(),
            P(DP, TP),
            P(DP, TP),
            P(DP, TP),
            P(TP, DP),
            P(DP, TP),
            P(DP, TP),
            P(TP, DP),
        ),
        check_vma=False,
    )
```

time: 1500 us -> 392 us (0.26)
  waiting for transfers between devices: 1260 us -> 143 us
  matrix products: 110 us -> 4.84 us
  Pallas kernels: 0 us -> 98.1 us
  starting transfers between devices: 10.6 us -> 54.1 us
  other arithmetic: 51.5 us -> 27.3 us
    unnamed x11 -> x4, waiting for transfers between devices: 451 us -> 0.07 us
    reduce_scatter x2, waiting for transfers between devices: 355 us -> 0.14 us  [the longest x1 0.14 us: per_device(): lax.psum_scatter(gate_up_term, ('y', 'z'), scatter_dimension=0, tiled=True)]
    all_gather x2, waiting for transfers between devices: 315 us -> 11.3 us  [gather_weights(): return lax.all_gather(own, ('y', 'z'), axis=0, tiled=True)]
    psum x3 -> x0, waiting for transfers between devices: 134 us -> none  [the longest x1 70.2 us: per_device(): branch = lax.psum(local_dot(attended, output_full), 'tensor')]
    ppermute x0 -> x50, waiting for transfers between devices: none -> 131 us  [swap(): return lambda value: lax.ppermute(value, axis, perm)]
    pallas_call x0 -> x38, Pallas kernels: none -> 98.1 us  [the longest x4 20.1 us: weight_grads(): pl.pallas_call(functools.partial(weight_grads_kernel, steps), grid=(count...]
    dot_general x20 -> x2, matrix products: 79.7 us -> 3.62 us  [local_dot(): return jnp.dot(left, right, preferred_element_type=f32)]
    ppermute x0 -> x50, starting transfers between devices: none -> 53.9 us  [swap(): return lambda value: lax.ppermute(value, axis, perm)]
  transfers between devices with their start and end apart: 10 -> 54, of which waited for: 9 -> 37; matrix products, arithmetic and copies ran while one was open for 8% -> 9% of each run, Pallas kernels for 0% -> 18%
where the time goes in v1:
time: 392 us; the launch traced here: 387 us
  waiting for transfers between devices  143 us (36%)
  Pallas kernels  98.1 us (25%)
  starting transfers between devices  54.1 us (14%)
  local copies, waits for them, and re-layouts  44.8 us (11%)
  other arithmetic  27.3 us (7%)
  between operations  15.3 us (4%)
  matrix products  4.84 us (1%)
    ppermute x50, waiting for transfers between devices, swap(): return lambda value: lax.ppermute(value, axis, perm)  131 us
    ppermute x50, starting transfers between devices, swap(): return lambda value: lax.ppermute(value, axis, perm)  53.9 us
    unnamed x130, local copies, waits for them, and re-layouts  39.1 us
    pallas_call x4, Pallas kernels, weight_grads(): pl.pallas_call(functools.partial(weight_grads_kernel, steps), grid=(count...  20.1 us
    pallas_call x3, Pallas kernels, to_width(): pl.pallas_call(to_width_kernel, grid=(4,), in_specs=[pl.BlockSpec(memory_...  20 us
    pallas_call x1, Pallas kernels, feed(): pl.pallas_call(feed_kernel, grid=(steps,), in_specs=[pl.BlockSpec((rows,...  15.8 us
    pallas_call x12, Pallas kernels, pack(): pl.pallas_call(functools.partial(pack_kernel, tuple(moves), len(pieces)),...  13.5 us
    all_gather x2, waiting for transfers between devices, gather_weights(): return lax.all_gather(own, ('y', 'z'), axis=0, tiled=True)  11.3 us
  transfers between devices with their start and end apart: 54, of which 37 were waited for; matrix products, arithmetic and copies ran while one was open for 9% of the time, Pallas kernels for 18%

profile of v1, /device:TPU:0, one launch (start us, length us, event | category | flops | bytes accessed | tf_op | source)
XLA Modules:
  0.0 387.1 jit_solution(11390792767717417820)
XLA Ops:
  10.7 2.1 collective-permute-start.5
  14.4 2.7 collective-permute-done.5
  17.9 2.3 choose.3
  20.3 2.2 collective-permute-start.18
  22.4 7.4 %collective-permute-done.17 = bf16[64,3072]{1,0:T(8,128)(2,1)S(1)} collective-permute-done((bf16[64,3072]{1,0:T(8,128)(2,1)}, bf16[64,3072]{1,0:T(8,128)(2,1)S(1)}, u32[]{:S(2)}, u32[]{:S(2)}) %collective-permute-start.17) | collective-permute-done | bytes 393248 | tf_op jit(solution)/shard_map/ppermute | solution.py:28
  35.2 2.1 collective-permute-start
  42.5 10.9 %collective-permute-done.2 = s32[4]{0:T(128)S(1)} collective-permute-done((s32[4]{0:T(128)S(1)}, s32[4]{0:T(128)S(1)}, u32[]{:S(2)}, u32[]{:S(2)}) %collective-permute-start.2) | collective-permute-done | bytes 48 | tf_op jit(solution)/shard_map/ppermute | solution.py:28
  53.9 2.4 fusion.13
  57.5 2.5 collective-permute-start.3
  66.9 2.4 fusion.2.value_ref
  69.3 10.2 %collective-permute-done.3.refs_1_ = bf16[192,2048]{1,0:T(8,128)(2,1)} collective-permute-done((bf16[192,2048]{1,0:T(8,128)(2,1)}, bf16[192,2048]{1,0:T(8,128)(2,1)}, u32[]{:S(2)}, u32[]{:S(2)}) %collective-permute-start.3) | collective-permute-done | bytes 786464 | tf_op jit(solution)/shard_map/ppermute | solution.py:28
  79.5 2.2 copy-done.30
  82.2 2.8 copy-done.14
  85.0 2.6 fusion.44
  87.7 5.3 %attend.1 = (bf16[2,2,192,768]{3,2,1,0:T(8,128)(2,1)S(1)}, bf16[2,2,192,256]{3,2,1,0:T(8,128)(2,1)S(1)}, f32[2,4,384]{2,1,0:T(4,128)S(1)}) custom-call(f32[2,2,192,768]{3,2,1,0:T(8,128)S(1)} %bitcast.43, f32[2,2,192,128]{3,2,1,0:T(8,128)S(1)} %bitcast.41, f32[2,2,192,128]{3,2,1,0:T(8,128)S(1)} %bitcast.39, f32[2,384,384]{2,1,0:T(8,128)S(1)} %copy-done.39), custom_call_target="tpu_custom_call" | custom-call | flops 754974720 | bytes 5898240 | tf_op jit(solution)/shard_map/attend/pallas_call | solution.py:391
  94.4 2.7 collective-permute-done.6.refs_1_
  97.6 2.0 collective-permute-start.7
  99.7 4.9 %collective-permute-done.9 = bf16[48,2048]{1,0:T(8,128)(2,1)S(1)} collective-permute-done((bf16[48,2048]{1,0:T(8,128)(2,1)S(1)}, bf16[48,2048]{1,0:T(8,128)(2,1)S(1)}, u32[]{:S(2)}, u32[]{:S(2)}) %collective-permute-start.9) | collective-permute-done | bytes 196640 | tf_op jit(solution)/shard_map/ppermute | solution.py:28
  105.4 2.0 collective-permute-start.10
  111.0 6.2 %collective-permute-done.10.far_ref = bf16[96,2048]{1,0:T(8,128)(2,1)} collective-permute-done((bf16[96,2048]{1,0:T(8,128)(2,1)}, bf16[96,2048]{1,0:T(8,128)(2,1)}, u32[]{:S(2)}, u32[]{:S(2)}) %collective-permute-start.10) | collective-permute-done | bytes 393248 | tf_op jit(solution)/shard_map/ppermute | solution.py:28
  122.2 2.0 copy-done.15
  127.3 2.5 pack.16.value_ref.cot_ref
  133.2 2.0 collective-permute-start.14
  135.3 2.1 collective-permute-start.15
  139.0 3.3 collective-permute-done.15.refs_3_
  143.5 3.4 collective-permute-done.16.refs_1_
  151.7 11.3 %all-gather.5.cloned.1.call-done.gate_up_ref.down_ref.full_ref = bf16[2048,3072]{1,0:T(8,128)(2,1)} async-done(((bf16[128,3072]{1,0:T(8,128)(2,1)}), bf16[2048,3072]{1,0:T(8,128)(2,1)}) %all-gather.5.cloned.1.call-update) | async-done | bytes 12582928 | tf_op jit(solution)/shard_map/all_gather | solution.py:208
  163.1 15.8 %feed.1 = (bf16[768,1024]{1,0:T(8,128)(2,1)S(1)}, bf16[768,2048]{1,0:T(8,128)(2,1)}) custom-call(bf16[768,2048]{1,0:T(8,128)(2,1)} %copy-done.13, bf16[768,2048]{1,0:T(8,128)(2,1)} %copy-done.6, bf16[2048,3072]{1,0:T(8,128)(2,1)} %all-gather.5.cloned.1.call-done.gate_up_ref.down_ref.full_ref, ...), custom_call_target="tpu_custom_call" | custom-call | flops 9663676416 | bytes 23592960 | tf_op jit(solution)/shard_map/feed/pallas_call | solution.py:549
  180.0 1.9 copy-done.57
  181.9 8.9 %weight_grads.4 = bf16[2048,2048]{1,0:T(8,128)(2,1)} custom-call(bf16[2048,768]{1,0:T(8,128)(2,1)S(1)} %copy-done.34, bf16[768,2048]{1,0:T(8,128)(2,1)S(1)} %copy-done.57), custom_call_target="tpu_custom_call" | custom-call | flops 6442450944 | bytes 14680064 | tf_op jit(solution)/shard_map/weight_grads/pallas_call | solution.py:513
  192.8 9.3 %to_width.3 = (bf16[384,2048]{1,0:T(8,128)(2,1)S(1)}, bf16[384,2048]{1,0:T(8,128)(2,1)S(1)}) custom-call(bf16[768,2048]{1,0:T(8,128)(2,1)S(1)} %copy-done.58, bf16[2048,3072]{1,0:T(8,128)(2,1)} %all-gather.5.cloned.1.call-done.gate_up_ref.down_ref.full_ref), custom_call_target="tpu_custom_call" | custom-call | flops 6442450944 | bytes 14680064 | tf_op jit(solution)/shard_map/to_width/pallas_call | solution.py:588
  202.1 5.1 %weight_grads.5.refs_0_ = bf16[2048,2048]{1,0:T(8,128)(2,1)} custom-call(bf16[2048,768]{1,0:T(8,128)(2,1)S(1)} %copy-done.17, bf16[768,1024]{1,0:T(8,128)(2,1)S(1)} %copy-done.24), custom_call_target="tpu_custom_call" | custom-call | flops 3221225472 | bytes 8912896 | tf_op jit(solution)/shard_map/weight_grads/pallas_call | solution.py:513
  211.3 2.1 collective-permute-start.21
  217.4 2.4 collective-permute-done.21
  221.0 2.2 collective-permute-start.23
  224.5 5.9 %to_width.4 = (bf16[384,4096]{1,0:T(8,128)(2,1)S(1)}, bf16[384,4096]{1,0:T(8,128)(2,1)S(1)}) custom-call(bf16[768,1024]{1,0:T(8,128)(2,1)S(1)} %copy-done.25, bf16[2048,3072]{1,0:T(8,128)(2,1)} %all-gather.5.cloned.1.call-done.gate_up_ref.down_ref.full_ref), custom_call_target="tpu_custom_call" | custom-call | flops 3221225472 | bytes 8912896 | tf_op jit(solution)/shard_map/to_width/pallas_call | solution.py:588
  232.7 1.9 collective-permute-done.22
  237.5 9.5 %collective-permute-done.25.refs_4_ = bf16[96,2048]{1,0:T(8,128)(2,1)S(1)} collective-permute-done((bf16[96,2048]{1,0:T(8,128)(2,1)S(1)}, bf16[96,2048]{1,0:T(8,128)(2,1)S(1)}, u32[]{:S(2)}, u32[]{:S(2)}) %collective-permute-start.25) | collective-permute-done | bytes 393248 | tf_op jit(solution)/shard_map/ppermute | solution.py:28
  247.2 2.3 collective-permute-start.27
  249.5 3.3 collective-permute-done.26.refs_2_
  255.6 3.4 collective-permute-done.28.refs_1_
  260.6 2.0 weight_grads.6.refs_0_
  264.4 6.0 %attend_back.1 = bf16[2,2,192,768]{3,2,1,0:T(8,128)(2,1)S(1)} custom-call(bf16[2,2,192,768]{3,2,1,0:T(8,128)(2,1)S(1)} %copy-done.54, bf16[2,2,192,256]{3,2,1,0:T(8,128)(2,1)S(1)} %bitcast.44, f32[2,4,384]{2,1,0:T(4,128)S(1)} %copy-done.56, f32[2,2,192,128]{3,2,1,0:T(8,128)S(1)} %bitcast.42, f32[2,2,192,128]{3,2,1,0:T(8,128)S(1)} %bitcast.40, ...), custom_call_target="tpu_custom_call" | custom-call | flops 2566914048 | bytes 5898240 | tf_op jit(solution)/shard_map/attend_back/pallas_call | solution.py:429
  270.4 4.1 %weight_grads.7 = bf16[2048,2048]{1,0:T(8,128)(2,1)} custom-call(bf16[2048,768]{1,0:T(8,128)(2,1)S(1)} %copy-done.12, bf16[768,768]{1,0:T(8,128)(2,1)S(1)} %bitcast.36, bf16[2048,2048]{1,0:T(8,128)(2,1)} %weight_grads.6.refs_0_), custom_call_target="tpu_custom_call", output_to_operand_aliasing={{}: (2, {})} | custom-call | flops 2415919104 | bytes 7471104 | tf_op jit(solution)/shard_map/weight_grads/pallas_call | solution.py:513
  280.8 4.9 %to_width.5 = (bf16[384,4096]{1,0:T(8,128)(2,1)S(1)}, bf16[384,4096]{1,0:T(8,128)(2,1)S(1)}) custom-call(bf16[768,768]{1,0:T(8,128)(2,1)S(1)} %bitcast.37, bf16[2048,768]{1,0:T(8,128)(2,1)} %copy-done.35, bf16[384,4096]{1,0:T(8,128)(2,1)S(1)} %copy-done.5, bf16[384,4096]{1,0:T(8,128)(2,1)S(1)} %copy-done.22), custom_call_target="tpu_custom_call", output_to_operand_aliasing={{0}: (2, {}), {1}: (3, {})} | custom-call | flops 2415919104 | bytes 7471104 | tf_op jit(solution)/shard_map/to_width/pallas_call | solution.py:588
  286.0 5.4 %collective-permute-done.29.refs_1_ = bf16[384,4096]{1,0:T(8,128)(2,1)S(1)} collective-permute-done((bf16[384,4096]{1,0:T(8,128)(2,1)S(1)}, bf16[384,4096]{1,0:T(8,128)(2,1)S(1)}, u32[]{:S(2)}, u32[]{:S(2)}) %collective-permute-start.29) | collective-permute-done | bytes 3145760 | tf_op jit(solution)/shard_map/ppermute | solution.py:28
  293.7 2.1 collective-permute-start.31
  295.8 3.8 fusion.3
  300.9 2.5 collective-permute-done.30
  303.4 2.4 collective-permute-done.31
  305.9 2.2 collective-permute-start.34
  309.6 2.9 collective-permute-start.36
  314.8 11.5 %collective-permute-done.37 = f32[2,2048]{1,0:T(2,128)S(1)} collective-permute-done((f32[2,2048]{1,0:T(2,128)S(1)}, f32[2,2048]{1,0:T(2,128)S(1)}, u32[]{:S(2)}, u32[]{:S(2)}) %collective-permute-start.37) | collective-permute-done | bytes 16416 | tf_op jit(solution)/shard_map/ppermute | solution.py:28
  328.7 2.8 collective-permute-start.41
  333.8 3.0 collective-permute-done.40
  336.8 8.7 %collective-permute-done.38.refs_1_ = bf16[96,4096]{1,0:T(8,128)(2,1)S(1)} collective-permute-done((bf16[96,4096]{1,0:T(8,128)(2,1)S(1)}, bf16[96,4096]{1,0:T(8,128)(2,1)S(1)}, u32[]{:S(2)}, u32[]{:S(2)}) %collective-permute-start.38) | collective-permute-done | bytes 786464 | tf_op jit(solution)/shard_map/ppermute | solution.py:28
  345.7 2.8 collective-permute-start.44
  348.6 2.0 collective-permute-start.47
  352.4 3.9 %collective-permute-done.43 = f32[2,2048]{1,0:T(2,128)S(1)} collective-permute-done((f32[2,2048]{1,0:T(2,128)S(1)}, f32[2,2048]{1,0:T(2,128)S(1)}, u32[]{:S(2)}, u32[]{:S(2)}) %collective-permute-start.43) | collective-permute-done | bytes 16416 | tf_op jit(solution)/shard_map/ppermute | solution.py:28
  356.3 2.0 collective-permute-done.47.other_ref
  358.7 2.0 pack.23
  364.2 2.2 fusion.7
  366.4 2.7 fusion.10
  372.4 6.4 %collective-permute-done.49.other_ref = bf16[64,2048]{1,0:T(8,128)(2,1)S(1)} collective-permute-done((bf16[64,2048]{1,0:T(8,128)(2,1)S(1)}, bf16[64,2048]{1,0:T(8,128)(2,1)S(1)}, u32[]{:S(2)}, u32[]{:S(2)}) %collective-permute-start.49) | collective-permute-done | bytes 262176 | tf_op jit(solution)/shard_map/ppermute | solution.py:28
  (294 shorter events, 105.0 us)
Async XLA Ops:
  7.2 72.3 %all-gather.3.cloned.1.call-start = ((), (), s32[]{:S(2)}) async-start(), calls=%async_computation.2 | async-start | bytes 4456448 | tf_op jit(solution)/shard_map/all_gather | solution.py:208
  7.2 25.1 %copy-start.2 = (bf16[384,2048]{1,0:T(8,128)(2,1)S(1)}, bf16[384,2048]{1,0:T(8,128)(2,1)}, u32[]{:S(2)}) copy-start(bf16[384,2048]{1,0:T(8,128)(2,1)} %value_ref) | copy-start | bytes 4718596
  9.0 5.4 %collective-permute-start.4 = (bf16[64,1024]{1,0:T(8,128)(2,1)}, bf16[64,1024]{1,0:T(8,128)(2,1)S(1)}, u32[]{:S(2)}, u32[]{:S(2)}) collective-permute-start(bf16[64,1024]{1,0:T(8,128)(2,1)} %get-tuple-element.124), channel_id=1, source_target_pairs={{0,2},{2,0},{16,18},{18,16},{1,3},{3,1},{17,19},{19,17},{4,6},{6,4... | collective-permute-start | bytes 393224 | tf_op jit(solution)/shard_map/ppermute | solution.py:28
  10.7 6.4 %collective-permute-start.5 = (bf16[64,1024]{1,0:T(8,128)(2,1)}, bf16[64,1024]{1,0:T(8,128)(2,1)S(1)}, u32[]{:S(2)}, u32[]{:S(2)}) collective-permute-start(bf16[64,1024]{1,0:T(8,128)(2,1)} %get-tuple-element.125), channel_id=1, source_target_pairs={{0,18},{2,16},{16,2},{18,0},{1,19},{3,17},{17,3},{19,1},{4,22},{6,... | collective-permute-start | bytes 393224 | tf_op jit(solution)/shard_map/ppermute | solution.py:28
  17.8 145.2 %all-gather.5.cloned.1.call-start = ((), (), s32[]{:S(2)}) async-start(), calls=%async_computation.3 | async-start | bytes 13369344 | tf_op jit(solution)/shard_map/all_gather | solution.py:208
  20.2 9.7 %collective-permute-start.17 = (bf16[64,3072]{1,0:T(8,128)(2,1)}, bf16[64,3072]{1,0:T(8,128)(2,1)S(1)}, u32[]{:S(2)}, u32[]{:S(2)}) collective-permute-start(bf16[64,3072]{1,0:T(8,128)(2,1)} %get-tuple-element.147), channel_id=1, source_target_pairs={{0,2},{2,0},{16,18},{18,16},{1,3},{3,1},{17,19},{19,17},{4,6},{6,4... | collective-permute-start | bytes 1179656 | tf_op jit(solution)/shard_map/ppermute | solution.py:28
  20.3 10.9 %collective-permute-start.18 = (bf16[64,3072]{1,0:T(8,128)(2,1)}, bf16[64,3072]{1,0:T(8,128)(2,1)S(1)}, u32[]{:S(2)}, u32[]{:S(2)}) collective-permute-start(bf16[64,3072]{1,0:T(8,128)(2,1)} %get-tuple-element.148), channel_id=1, source_target_pairs={{0,18},{2,16},{16,2},{18,0},{1,19},{3,17},{17,3},{19,1},{4,22},{6,... | collective-permute-start | bytes 1179656 | tf_op jit(solution)/shard_map/ppermute | solution.py:28
  32.2 243.5 %reduce-scatter.3.cloned.1.call-start = ((), (), s32[]{:S(2)}) async-start(), calls=%async_computation.4 | async-start | bytes 8912896 | tf_op jit(solution)/shard_map/reduce_scatter | solution.py:752
  35.2 18.4 %collective-permute-start = (bf16[192,2048]{1,0:T(8,128)(2,1)S(1)}, bf16[192,2048]{1,0:T(8,128)(2,1)S(1)}, u32[]{:S(2)}, u32[]{:S(2)}) collective-permute-start(bf16[192,2048]{1,0:T(8,128)(2,1)S(1)} %pack.12), channel_id=1, source_target_pairs={{0,18},{2,16},{16,2},{18,0},{1,19},{3,17},{17,3},{19,1},{4,22},{6,... | collective-permute-start | bytes 2359304 | tf_op jit(solution)/shard_map/ppermute | solution.py:28
  37.3 16.1 %collective-permute-start.2 = (s32[4]{0:T(128)S(1)}, s32[4]{0:T(128)S(1)}, u32[]{:S(2)}, u32[]{:S(2)}) collective-permute-start(s32[4]{0:T(128)S(1)} %copy-done.64), channel_id=1, source_target_pairs={{0,18},{2,16},{16,2},{18,0},{1,19},{3,17},{17,3},{19,1},{4,22},{6,... | collective-permute-start | bytes 56 | tf_op jit(solution)/shard_map/ppermute | solution.py:28
  53.6 6.5 %collective-permute-start.1 = (bf16[192,2048]{1,0:T(8,128)(2,1)S(1)}, bf16[192,2048]{1,0:T(8,128)(2,1)S(1)}, u32[]{:S(2)}, u32[]{:S(2)}) collective-permute-start(bf16[192,2048]{1,0:T(8,128)(2,1)S(1)} %collective-permute-done.refs_1_), channel_id=1, source_target_pairs={{0,1},{1,0},{2,3},{3,2},{4,5},{5,4},{6,7},{7,6},{8,9},{9,8},{10,11... | collective-permute-start | bytes 2359304 | tf_op jit(solution)/shard_map/ppermute | solution.py:28
  56.3 31.4 %copy-start.45 = (f32[768,128]{1,0:T(8,128)}, f32[768,128]{1,0:T(8,128)S(1)}, u32[]{:S(2)}) copy-start(f32[768,128]{1,0:T(8,128)S(1)} %get-tuple-element.128) | copy-start | bytes 1179652
  57.5 21.9 %collective-permute-start.3 = (bf16[192,2048]{1,0:T(8,128)(2,1)}, bf16[192,2048]{1,0:T(8,128)(2,1)}, u32[]{:S(2)}, u32[]{:S(2)}) collective-permute-start(bf16[192,2048]{1,0:T(8,128)(2,1)} %pack.13), channel_id=1, source_target_pairs={{0,18},{2,16},{16,2},{18,0},{1,19},{3,17},{17,3},{19,1},{4,22},{6,... | collective-permute-start | bytes 2359304 | tf_op jit(solution)/shard_map/ppermute | solution.py:28
  82.2 11.5 %copy-start.31 = (bf16[2048,256]{1,0:T(8,128)(2,1)}, bf16[2048,256]{1,0:T(8,128)(2,1)S(1)}, u32[]{:S(2)}) copy-start(bf16[2048,256]{1,0:T(8,128)(2,1)S(1)} %get-tuple-element.131) | copy-start | bytes 3145732
  93.7 3.5 collective-permute-start.6
  94.4 13.7 %copy-start.63 = (f32[2048]{0:T(1024)S(1)}, f32[2048]{0:T(1024)}, u32[]{:S(2)}) copy-start(f32[2048]{0:T(1024)} %param.15) | copy-start | bytes 24580
  97.5 7.0 %collective-permute-start.9 = (bf16[48,2048]{1,0:T(8,128)(2,1)S(1)}, bf16[48,2048]{1,0:T(8,128)(2,1)S(1)}, u32[]{:S(2)}, u32[]{:S(2)}) collective-permute-start(bf16[48,2048]{1,0:T(8,128)(2,1)S(1)} %get-tuple-element.136), channel_id=1, source_target_pairs={{0,2},{2,0},{16,18},{18,16},{1,3},{3,1},{17,19},{19,17},{4,6},{6,4... | collective-permute-start | bytes 589832 | tf_op jit(solution)/shard_map/ppermute | solution.py:28
  97.6 9.7 %collective-permute-start.7 = (bf16[48,2048]{1,0:T(8,128)(2,1)S(1)}, bf16[48,2048]{1,0:T(8,128)(2,1)S(1)}, u32[]{:S(2)}, u32[]{:S(2)}) collective-permute-start(bf16[48,2048]{1,0:T(8,128)(2,1)S(1)} %get-tuple-element.134), channel_id=1, source_target_pairs={{0,18},{2,16},{16,2},{18,0},{1,19},{3,17},{17,3},{19,1},{4,22},{6,... | collective-permute-start | bytes 589832 | tf_op jit(solution)/shard_map/ppermute | solution.py:28
  105.4 11.9 %collective-permute-start.10 = (bf16[96,2048]{1,0:T(8,128)(2,1)}, bf16[96,2048]{1,0:T(8,128)(2,1)}, u32[]{:S(2)}, u32[]{:S(2)}) collective-permute-start(bf16[96,2048]{1,0:T(8,128)(2,1)} %pad_maximum_fusion.5), channel_id=1, source_target_pairs={{0,18},{2,16},{16,2},{18,0},{1,19},{3,17},{17,3},{19,1},{4,22},{6,... | collective-permute-start | bytes 1179656 | tf_op jit(solution)/shard_map/ppermute | solution.py:28
  108.2 10.4 %collective-permute-start.8 = (bf16[96,2048]{1,0:T(8,128)(2,1)}, bf16[96,2048]{1,0:T(8,128)(2,1)}, u32[]{:S(2)}, u32[]{:S(2)}) collective-permute-start(bf16[96,2048]{1,0:T(8,128)(2,1)} %pad_maximum_fusion.4), channel_id=1, source_target_pairs={{0,2},{2,0},{16,18},{18,16},{1,3},{3,1},{17,19},{19,17},{4,6},{6,4... | collective-permute-start | bytes 1179656 | tf_op jit(solution)/shard_map/ppermute | solution.py:28
  108.2 19.1 %collective-permute-start.11 = (bf16[192,2048]{1,0:T(8,128)(2,1)}, bf16[192,2048]{1,0:T(8,128)(2,1)}, u32[]{:S(2)}, u32[]{:S(2)}) collective-permute-start(bf16[192,2048]{1,0:T(8,128)(2,1)} %collective-permute-done.3.refs_1_), channel_id=1, source_target_pairs={{0,1},{1,0},{2,3},{3,2},{4,5},{5,4},{6,7},{7,6},{8,9},{9,8},{10,11... | collective-permute-start | bytes 2359304 | tf_op jit(solution)/shard_map/ppermute | solution.py:28
  120.9 12.3 %collective-permute-start.13 = (bf16[96,2048]{1,0:T(8,128)(2,1)S(1)}, bf16[96,2048]{1,0:T(8,128)(2,1)S(1)}, u32[]{:S(2)}, u32[]{:S(2)}) collective-permute-start(bf16[96,2048]{1,0:T(8,128)(2,1)S(1)} %get-tuple-element.140.refs_0_), channel_id=1, source_target_pairs={{0,18},{2,16},{16,2},{18,0},{1,19},{3,17},{17,3},{19,1},{4,22},{6,... | collective-permute-start | bytes 1179656 | tf_op jit(solution)/shard_map/ppermute | solution.py:28
  122.2 11.0 %collective-permute-start.12 = (bf16[96,2048]{1,0:T(8,128)(2,1)S(1)}, bf16[96,2048]{1,0:T(8,128)(2,1)S(1)}, u32[]{:S(2)}, u32[]{:S(2)}) collective-permute-start(bf16[96,2048]{1,0:T(8,128)(2,1)S(1)} %get-tuple-element.140.refs_0_), channel_id=1, source_target_pairs={{0,2},{2,0},{16,18},{18,16},{1,3},{3,1},{17,19},{19,17},{4,6},{6,4... | collective-permute-start | bytes 1179656 | tf_op jit(solution)/shard_map/ppermute | solution.py:28
  133.2 5.7 %collective-permute-start.14 = (bf16[48,2048]{1,0:T(8,128)(2,1)S(1)}, bf16[48,2048]{1,0:T(8,128)(2,1)S(1)}, u32[]{:S(2)}, u32[]{:S(2)}) collective-permute-start(bf16[48,2048]{1,0:T(8,128)(2,1)S(1)} %slice.107), channel_id=1, source_target_pairs={{0,2},{2,0},{16,18},{18,16},{1,3},{3,1},{17,19},{19,17},{4,6},{6,4... | collective-permute-start | bytes 589832 | tf_op jit(solution)/shard_map/ppermute | solution.py:28
  135.3 7.0 %collective-permute-start.15 = (bf16[48,2048]{1,0:T(8,128)(2,1)S(1)}, bf16[48,2048]{1,0:T(8,128)(2,1)S(1)}, u32[]{:S(2)}, u32[]{:S(2)}) collective-permute-start(bf16[48,2048]{1,0:T(8,128)(2,1)S(1)} %slice.108), channel_id=1, source_target_pairs={{0,18},{2,16},{16,2},{18,0},{1,19},{3,17},{17,3},{19,1},{4,22},{6,... | collective-permute-start | bytes 589832 | tf_op jit(solution)/shard_map/ppermute | solution.py:28
  143.4 3.5 collective-permute-start.16
  163.1 17.0 %copy-start.34 = (bf16[2048,768]{1,0:T(8,128)(2,1)S(1)}, bf16[2048,768]{1,0:T(8,128)(2,1)}, u32[]{:S(2)}) copy-start(bf16[2048,768]{1,0:T(8,128)(2,1)} %copy-done.33) | copy-start | bytes 9437188
  190.8 178.3 %reduce-scatter.5.cloned.1.call-start = ((), (), s32[]{:S(2)}) async-start(), calls=%async_computation.5 | async-start | bytes 8912896 | tf_op jit(solution)/shard_map/reduce_scatter | solution.py:789
  202.0 5.2 %collective-permute-start.19 = (bf16[384,2048]{1,0:T(8,128)(2,1)S(1)}, bf16[384,2048]{1,0:T(8,128)(2,1)S(1)}, u32[]{:S(2)}, u32[]{:S(2)}) collective-permute-start(bf16[384,2048]{1,0:T(8,128)(2,1)S(1)} %get-tuple-element.157), channel_id=1, source_target_pairs={{0,1},{1,0},{2,3},{3,2},{4,5},{5,4},{6,7},{7,6},{8,9},{9,8},{10,11... | collective-permute-start | bytes 4718600 | tf_op jit(solution)/shard_map/ppermute | solution.py:28
  209.8 7.6 %collective-permute-start.20 = (bf16[48,2048]{1,0:T(8,128)(2,1)}, bf16[48,2048]{1,0:T(8,128)(2,1)}, u32[]{:S(2)}, u32[]{:S(2)}) collective-permute-start(bf16[48,2048]{1,0:T(8,128)(2,1)} %get-tuple-element.163), channel_id=1, source_target_pairs={{0,2},{2,0},{16,18},{18,16},{1,3},{3,1},{17,19},{19,17},{4,6},{6,4... | collective-permute-start | bytes 589832 | tf_op jit(solution)/shard_map/ppermute | solution.py:28
  211.3 8.5 %collective-permute-start.21 = (bf16[48,2048]{1,0:T(8,128)(2,1)}, bf16[48,2048]{1,0:T(8,128)(2,1)}, u32[]{:S(2)}, u32[]{:S(2)}) collective-permute-start(bf16[48,2048]{1,0:T(8,128)(2,1)} %get-tuple-element.164), channel_id=1, source_target_pairs={{0,18},{2,16},{16,2},{18,0},{1,19},{3,17},{17,3},{19,1},{4,22},{6,... | collective-permute-start | bytes 589832 | tf_op jit(solution)/shard_map/ppermute | solution.py:28
  221.0 11.7 %collective-permute-start.23 = (bf16[96,2048]{1,0:T(8,128)(2,1)S(1)}, bf16[96,2048]{1,0:T(8,128)(2,1)S(1)}, u32[]{:S(2)}, u32[]{:S(2)}) collective-permute-start(bf16[96,2048]{1,0:T(8,128)(2,1)S(1)} %pad_maximum_fusion.7), channel_id=1, source_target_pairs={{0,18},{2,16},{16,2},{18,0},{1,19},{3,17},{17,3},{19,1},{4,22},{6,... | collective-permute-start | bytes 1179656 | tf_op jit(solution)/shard_map/ppermute | solution.py:28
  224.4 10.3 %collective-permute-start.22 = (bf16[96,2048]{1,0:T(8,128)(2,1)S(1)}, bf16[96,2048]{1,0:T(8,128)(2,1)S(1)}, u32[]{:S(2)}, u32[]{:S(2)}) collective-permute-start(bf16[96,2048]{1,0:T(8,128)(2,1)S(1)} %pad_maximum_fusion.6), channel_id=1, source_target_pairs={{0,2},{2,0},{16,18},{18,16},{1,3},{3,1},{17,19},{19,17},{4,6},{6,4... | collective-permute-start | bytes 1179656 | tf_op jit(solution)/shard_map/ppermute | solution.py:28
  232.0 23.2 %copy-start.4 = (bf16[384,4096]{1,0:T(8,128)(2,1)}, bf16[384,4096]{1,0:T(8,128)(2,1)S(1)}, u32[]{:S(2)}) copy-start(bf16[384,4096]{1,0:T(8,128)(2,1)S(1)} %get-tuple-element.177.refs_0_) | copy-start | bytes 9437188
  236.4 10.6 %collective-permute-start.25 = (bf16[96,2048]{1,0:T(8,128)(2,1)S(1)}, bf16[96,2048]{1,0:T(8,128)(2,1)S(1)}, u32[]{:S(2)}, u32[]{:S(2)}) collective-permute-start(bf16[96,2048]{1,0:T(8,128)(2,1)S(1)} %add_convert_fusion.refs_0_), channel_id=1, source_target_pairs={{0,18},{2,16},{16,2},{18,0},{1,19},{3,17},{17,3},{19,1},{4,22},{6,... | collective-permute-start | bytes 1179656 | tf_op jit(solution)/shard_map/ppermute | solution.py:28
  237.5 9.6 %collective-permute-start.24 = (bf16[96,2048]{1,0:T(8,128)(2,1)S(1)}, bf16[96,2048]{1,0:T(8,128)(2,1)S(1)}, u32[]{:S(2)}, u32[]{:S(2)}) collective-permute-start(bf16[96,2048]{1,0:T(8,128)(2,1)S(1)} %add_convert_fusion.refs_0_), channel_id=1, source_target_pairs={{0,2},{2,0},{16,18},{18,16},{1,3},{3,1},{17,19},{19,17},{4,6},{6,4... | collective-permute-start | bytes 1179656 | tf_op jit(solution)/shard_map/ppermute | solution.py:28
  247.0 5.7 %collective-permute-start.26 = (bf16[48,2048]{1,0:T(8,128)(2,1)S(1)}, bf16[48,2048]{1,0:T(8,128)(2,1)S(1)}, u32[]{:S(2)}, u32[]{:S(2)}) collective-permute-start(bf16[48,2048]{1,0:T(8,128)(2,1)S(1)} %slice.131), channel_id=1, source_target_pairs={{0,2},{2,0},{16,18},{18,16},{1,3},{3,1},{17,19},{19,17},{4,6},{6,4... | collective-permute-start | bytes 589832 | tf_op jit(solution)/shard_map/ppermute | solution.py:28
  247.2 7.0 %collective-permute-start.27 = (bf16[48,2048]{1,0:T(8,128)(2,1)S(1)}, bf16[48,2048]{1,0:T(8,128)(2,1)S(1)}, u32[]{:S(2)}, u32[]{:S(2)}) collective-permute-start(bf16[48,2048]{1,0:T(8,128)(2,1)S(1)} %slice.132), channel_id=1, source_target_pairs={{0,18},{2,16},{16,2},{18,0},{1,19},{3,17},{17,3},{19,1},{4,22},{6,... | collective-permute-start | bytes 589832 | tf_op jit(solution)/shard_map/ppermute | solution.py:28
  255.3 3.7 collective-permute-start.28
  285.7 5.7 %collective-permute-start.29 = (bf16[384,4096]{1,0:T(8,128)(2,1)S(1)}, bf16[384,4096]{1,0:T(8,128)(2,1)S(1)}, u32[]{:S(2)}, u32[]{:S(2)}) collective-permute-start(bf16[384,4096]{1,0:T(8,128)(2,1)S(1)} %get-tuple-element.180), channel_id=1, source_target_pairs={{0,1},{1,0},{2,3},{3,2},{4,5},{5,4},{6,7},{7,6},{8,9},{9,8},{10,11... | collective-permute-start | bytes 9437192 | tf_op jit(solution)/shard_map/ppermute | solution.py:28
  292.2 11.2 %collective-permute-start.30 = (bf16[48,4096]{1,0:T(8,128)(2,1)S(1)}, bf16[48,4096]{1,0:T(8,128)(2,1)S(1)}, u32[]{:S(2)}, u32[]{:S(2)}) collective-permute-start(bf16[48,4096]{1,0:T(8,128)(2,1)S(1)} %get-tuple-element.183), channel_id=1, source_target_pairs={{0,2},{2,0},{16,18},{18,16},{1,3},{3,1},{17,19},{19,17},{4,6},{6,4... | collective-permute-start | bytes 1179656 | tf_op jit(solution)/shard_map/ppermute | solution.py:28
  293.7 12.1 %collective-permute-start.31 = (bf16[48,4096]{1,0:T(8,128)(2,1)S(1)}, bf16[48,4096]{1,0:T(8,128)(2,1)S(1)}, u32[]{:S(2)}, u32[]{:S(2)}) collective-permute-start(bf16[48,4096]{1,0:T(8,128)(2,1)S(1)} %get-tuple-element.184), channel_id=1, source_target_pairs={{0,18},{2,16},{16,2},{18,0},{1,19},{3,17},{17,3},{19,1},{4,22},{6,... | collective-permute-start | bytes 1179656 | tf_op jit(solution)/shard_map/ppermute | solution.py:28
  299.6 1.3 collective-permute-start.32
  305.9 21.8 %collective-permute-start.34 = (bf16[96,4096]{1,0:T(8,128)(2,1)S(1)}, bf16[96,4096]{1,0:T(8,128)(2,1)S(1)}, u32[]{:S(2)}, u32[]{:S(2)}) collective-permute-start(bf16[96,4096]{1,0:T(8,128)(2,1)S(1)} %pad_maximum_fusion.2), channel_id=1, source_target_pairs={{0,18},{2,16},{16,2},{18,0},{1,19},{3,17},{17,3},{19,1},{4,22},{6,... | collective-permute-start | bytes 2359304 | tf_op jit(solution)/shard_map/ppermute | solution.py:28
  308.2 19.5 %collective-permute-start.33 = (bf16[96,4096]{1,0:T(8,128)(2,1)S(1)}, bf16[96,4096]{1,0:T(8,128)(2,1)S(1)}, u32[]{:S(2)}, u32[]{:S(2)}) collective-permute-start(bf16[96,4096]{1,0:T(8,128)(2,1)S(1)} %pad_maximum_fusion.1), channel_id=1, source_target_pairs={{0,2},{2,0},{16,18},{18,16},{1,3},{3,1},{17,19},{19,17},{4,6},{6,4... | collective-permute-start | bytes 2359304 | tf_op jit(solution)/shard_map/ppermute | solution.py:28
  308.3 17.9 %collective-permute-start.37 = (f32[2,2048]{1,0:T(2,128)S(1)}, f32[2,2048]{1,0:T(2,128)S(1)}, u32[]{:S(2)}, u32[]{:S(2)}) collective-permute-start(f32[2,2048]{1,0:T(2,128)S(1)} %fusion.38), channel_id=1, source_target_pairs={{0,18},{2,16},{16,2},{18,0},{1,19},{3,17},{17,3},{19,1},{4,22},{6,... | collective-permute-start | bytes 49160 | tf_op jit(solution)/shard_map/ppermute | solution.py:28
  309.6 18.1 %collective-permute-start.36 = (f32[2,2048]{1,0:T(2,128)S(1)}, f32[2,2048]{1,0:T(2,128)S(1)}, u32[]{:S(2)}, u32[]{:S(2)}) collective-permute-start(f32[2,2048]{1,0:T(2,128)S(1)} %fusion.38), channel_id=1, source_target_pairs={{0,16},{2,18},{16,0},{18,2},{1,17},{3,19},{17,1},{19,3},{4,20},{6,... | collective-permute-start | bytes 49160 | tf_op jit(solution)/shard_map/ppermute | solution.py:28
  312.5 15.2 %collective-permute-start.35 = (f32[2,2048]{1,0:T(2,128)S(1)}, f32[2,2048]{1,0:T(2,128)S(1)}, u32[]{:S(2)}, u32[]{:S(2)}) collective-permute-start(f32[2,2048]{1,0:T(2,128)S(1)} %fusion.38), channel_id=1, source_target_pairs={{0,2},{2,0},{16,18},{18,16},{1,3},{3,1},{17,19},{19,17},{4,6},{6,4... | collective-permute-start | bytes 49160 | tf_op jit(solution)/shard_map/ppermute | solution.py:28
  314.8 13.2 %copy-start.20 = (f32[96,2048]{1,0:T(8,128)S(1)}, f32[96,2048]{1,0:T(8,128)}, u32[]{:S(2)}) copy-start(f32[96,2048]{1,0:T(8,128)} %copy-done.18) | copy-start | bytes 2359300
  328.1 20.4 %copy-start.59 = (bf16[128,2048]{1,0:T(8,128)(2,1)S(1)}, bf16[128,2048]{1,0:T(8,128)(2,1)}, u32[]{:S(2)}) copy-start(bf16[128,2048]{1,0:T(8,128)(2,1)} %reduce-scatter.3.cloned.1.call-done) | copy-start | bytes 1572868
  328.2 22.4 %copy-start.3 = (bf16[384,2048]{1,0:T(8,128)(2,1)S(1)}, bf16[384,2048]{1,0:T(8,128)(2,1)}, u32[]{:S(2)}) copy-start(bf16[384,2048]{1,0:T(8,128)(2,1)} %value_ref) | copy-start | bytes 4718596
  328.5 16.9 %collective-permute-start.38 = (bf16[96,4096]{1,0:T(8,128)(2,1)S(1)}, bf16[96,4096]{1,0:T(8,128)(2,1)S(1)}, u32[]{:S(2)}, u32[]{:S(2)}) collective-permute-start(bf16[96,4096]{1,0:T(8,128)(2,1)S(1)} %turned.7.refs_0_), channel_id=1, source_target_pairs={{0,2},{2,0},{16,18},{18,16},{1,3},{3,1},{17,19},{19,17},{4,6},{6,4... | collective-permute-start | bytes 2359304 | tf_op jit(solution)/shard_map/ppermute | solution.py:28
  328.7 5.1 %collective-permute-start.41 = (f32[2,2048]{1,0:T(2,128)S(1)}, f32[2,2048]{1,0:T(2,128)S(1)}, u32[]{:S(2)}, u32[]{:S(2)}) collective-permute-start(f32[2,2048]{1,0:T(2,128)S(1)} %add_add_fusion.2), channel_id=1, source_target_pairs={{0,96},{32,64},{64,32},{96,0},{1,97},{33,65},{65,33},{97,1},{2,98}... | collective-permute-start | bytes 49160 | tf_op jit(solution)/shard_map/ppermute | solution.py:28
  331.4 5.4 %collective-permute-start.40 = (f32[2,2048]{1,0:T(2,128)S(1)}, f32[2,2048]{1,0:T(2,128)S(1)}, u32[]{:S(2)}, u32[]{:S(2)}) collective-permute-start(f32[2,2048]{1,0:T(2,128)S(1)} %add_add_fusion.2), channel_id=1, source_target_pairs={{0,64},{32,96},{64,0},{96,32},{1,65},{33,97},{65,1},{97,33},{2,66}... | collective-permute-start | bytes 49160 | tf_op jit(solution)/shard_map/ppermute | solution.py:28
  332.3 4.5 %collective-permute-start.39 = (f32[2,2048]{1,0:T(2,128)S(1)}, f32[2,2048]{1,0:T(2,128)S(1)}, u32[]{:S(2)}, u32[]{:S(2)}) collective-permute-start(f32[2,2048]{1,0:T(2,128)S(1)} %add_add_fusion.2), channel_id=1, source_target_pairs={{0,32},{32,0},{64,96},{96,64},{1,33},{33,1},{65,97},{97,65},{2,34}... | collective-permute-start | bytes 49160 | tf_op jit(solution)/shard_map/ppermute | solution.py:28
  345.6 10.7 %collective-permute-start.45 = (bf16[192,4096]{1,0:T(8,128)(2,1)S(1)}, bf16[192,4096]{1,0:T(8,128)(2,1)S(1)}, u32[]{:S(2)}, u32[]{:S(2)}) collective-permute-start(bf16[192,4096]{1,0:T(8,128)(2,1)S(1)} %pack.22), channel_id=1, source_target_pairs={{0,1},{1,0},{2,3},{3,2},{4,5},{5,4},{6,7},{7,6},{8,9},{9,8},{10,11... | collective-permute-start | bytes 4718600 | tf_op jit(solution)/shard_map/ppermute | solution.py:28
  345.7 18.5 %copy-start.62 = (f32[2048]{0:T(1024)S(1)}, f32[2048]{0:T(1024)}, u32[]{:S(2)}) copy-start(f32[2048]{0:T(1024)} %param.14) | copy-start | bytes 24580
  345.7 6.4 %collective-permute-start.44 = (f32[2,2048]{1,0:T(2,128)S(1)}, f32[2,2048]{1,0:T(2,128)S(1)}, u32[]{:S(2)}, u32[]{:S(2)}) collective-permute-start(f32[2,2048]{1,0:T(2,128)S(1)} %add_add_fusion.1), channel_id=1, source_target_pairs={{0,12},{4,8},{8,4},{12,0},{1,13},{5,9},{9,5},{13,1},{2,14},{6,10},... | collective-permute-start | bytes 49160 | tf_op jit(solution)/shard_map/ppermute | solution.py:28
  348.6 9.7 %collective-permute-start.47 = (bf16[64,2048]{1,0:T(8,128)(2,1)S(1)}, bf16[64,2048]{1,0:T(8,128)(2,1)S(1)}, u32[]{:S(2)}, u32[]{:S(2)}) collective-permute-start(bf16[64,2048]{1,0:T(8,128)(2,1)S(1)} %get-tuple-element.235), channel_id=1, source_target_pairs={{0,18},{2,16},{16,2},{18,0},{1,19},{3,17},{17,3},{19,1},{4,22},{6,... | collective-permute-start | bytes 786440 | tf_op jit(solution)/shard_map/ppermute | solution.py:28
  350.6 8.1 %collective-permute-start.46 = (bf16[64,2048]{1,0:T(8,128)(2,1)S(1)}, bf16[64,2048]{1,0:T(8,128)(2,1)S(1)}, u32[]{:S(2)}, u32[]{:S(2)}) collective-permute-start(bf16[64,2048]{1,0:T(8,128)(2,1)S(1)} %get-tuple-element.236), channel_id=1, source_target_pairs={{0,2},{2,0},{16,18},{18,16},{1,3},{3,1},{17,19},{19,17},{4,6},{6,4... | collective-permute-start | bytes 786440 | tf_op jit(solution)/shard_map/ppermute | solution.py:28
  350.9 5.3 %collective-permute-start.43 = (f32[2,2048]{1,0:T(2,128)S(1)}, f32[2,2048]{1,0:T(2,128)S(1)}, u32[]{:S(2)}, u32[]{:S(2)}) collective-permute-start(f32[2,2048]{1,0:T(2,128)S(1)} %add_add_fusion.1), channel_id=1, source_target_pairs={{0,8},{4,12},{8,0},{12,4},{1,9},{5,13},{9,1},{13,5},{2,10},{6,14},... | collective-permute-start | bytes 49160 | tf_op jit(solution)/shard_map/ppermute | solution.py:28
  352.1 4.2 %collective-permute-start.42 = (f32[2,2048]{1,0:T(2,128)S(1)}, f32[2,2048]{1,0:T(2,128)S(1)}, u32[]{:S(2)}, u32[]{:S(2)}) collective-permute-start(f32[2,2048]{1,0:T(2,128)S(1)} %add_add_fusion.1), channel_id=1, source_target_pairs={{0,4},{4,0},{8,12},{12,8},{1,5},{5,1},{9,13},{13,9},{2,6},{6,2},{1... | collective-permute-start | bytes 49160 | tf_op jit(solution)/shard_map/ppermute | solution.py:28
  370.2 8.7 %collective-permute-start.49 = (bf16[64,2048]{1,0:T(8,128)(2,1)S(1)}, bf16[64,2048]{1,0:T(8,128)(2,1)S(1)}, u32[]{:S(2)}, u32[]{:S(2)}) collective-permute-start(bf16[64,2048]{1,0:T(8,128)(2,1)S(1)} %get-tuple-element.233), channel_id=1, source_target_pairs={{0,18},{2,16},{16,2},{18,0},{1,19},{3,17},{17,3},{19,1},{4,22},{6,... | collective-permute-start | bytes 786440 | tf_op jit(solution)/shard_map/ppermute | solution.py:28
  371.8 7.4 %collective-permute-start.48 = (bf16[64,2048]{1,0:T(8,128)(2,1)S(1)}, bf16[64,2048]{1,0:T(8,128)(2,1)S(1)}, u32[]{:S(2)}, u32[]{:S(2)}) collective-permute-start(bf16[64,2048]{1,0:T(8,128)(2,1)S(1)} %get-tuple-element.234), channel_id=1, source_target_pairs={{0,2},{2,0},{16,18},{18,16},{1,3},{3,1},{17,19},{19,17},{4,6},{6,4... | collective-permute-start | bytes 786440 | tf_op jit(solution)/shard_map/ppermute | solution.py:28
  (55 other events, 168.1 us)
Sparse Core Ops, SparseCore 0:
  17.9 53.1 all-gather.2
  73.3 89.7 all-gather.4
  190.9 84.7 reduce-scatter.2
  279.0 84.7 reduce-scatter.4
